TPU v7x, 32 devices: a whole 2x2x4 slice. The times are simulated.
32 devices in a mesh: grp: 1, row: 8 (over y, x, core), sub: 4 (over z).
Axes of the slice: x: 2, y: 2, z: 4, core: 2. Of those that a mesh axis runs over, the one named last changes fastest.
Arguments:
- pair: bfloat16 [128, 128, 128], P(('grp', 'row', 'sub')), may hold values from -6 to 6
- mask: int32 [128], P('grp'), may hold values from 0 to 1, as said below
- chain: int32 [128], P('grp'), may hold values from 0 to 3, never falling along the last dimension, each value on 1 to 64 neighbouring positions
- ln_gain: float32 [2, 128], replicated, may hold values from 0.5 to 1.5
- ln_shift: float32 [2, 128], replicated, may hold values from -2 to 2
- w_qkvg: bfloat16 [2, 128, 512], replicated, may hold values from -0.5 to 0.5
- gate_bias: float32 [2, 128], replicated, may hold values from -4 to 4
- w_bias: bfloat16 [2, 4, 128], replicated, may hold values from -1 to 1
- w_out: bfloat16 [2, 128, 128], replicated, may hold values from -0.5 to 0.5
- out_bias: float32 [2, 128], replicated, may hold values from -2 to 2
- chain_offset: float32 [2, 4], replicated, may hold values from -300 to 300
Outputs:
- pair_out: bfloat16 [128, 128, 128], P('grp', ('row', 'sub'))
Inputs may be any that keep to these rules, and one draw needn't show every extreme that they name: mask[r] is 1 for r below some L with 64 <= L < 128, and 0 for the rest.
All inputs are finite; a program needn't handle non-finite values.
Results may differ from a plain program's by a relative error of at most 0.0061.
Values may be sent and summed in bfloat16 or wider, within the bound.
No kernel may reach another device: no remote copies, remote signals or barrier semaphores. Data moves between devices by JAX's collectives and lax.ppermute only.
A program may use at most 64 MiB of HBM per device.

v0:
```python
import math

import jax
import jax.numpy as jnp
from jax import lax
from jax.sharding import PartitionSpec as P

C = 128
HEADS = 4
HEAD_DIM = 32
HD = 128


EPS = 1e-05


def layer_norm(entries, gain_row, shift_row):
    values = entries.astype(jnp.float32)
    middle = jnp.mean(values, axis=-1, keepdims=True)
    spread = jnp.mean(jnp.square(values - middle), axis=-1, keepdims=True)
    return ((values - middle) * lax.rsqrt(spread + EPS) * gain_row + shift_row).astype(jnp.bfloat16)


def softmax_weights(logits):
    maximum = jnp.max(logits, axis=-1, keepdims=True)
    expon = jnp.exp(logits - maximum)
    return (expon / jnp.sum(expon, axis=-1, keepdims=True)).astype(jnp.bfloat16)


def project(normed, weights):
    column_scale = jnp.where(jnp.arange(4 * HD) < HD, HEAD_DIM ** (-0.5), 1.0).astype(jnp.float32)
    flattened = normed.reshape(-1, normed.shape[-1])
    projected = jnp.dot(flattened, weights, preferred_element_type=jnp.float32) * column_scale
    return projected.astype(jnp.bfloat16).reshape(normed.shape[0], normed.shape[1], 4 * HD)


def local(
    pair, mask, chain, ln_gain, ln_shift, w_qkvg, gate_bias, w_bias, w_out, out_bias, chain_offset
):
    row_count = pair.shape[0]
    residues = pair.shape[1]
    outer = lax.axis_size("row")
    span = residues // outer
    step_cap = max(1, 64 // outer)
    key_mask = jnp.where(mask > 0, 0.0, -1000000000.0).astype(jnp.float32)
    chain_grid = chain.reshape(outer, span)
    normed = layer_norm(pair, ln_gain[0], ln_shift[0])
    projected = project(normed, w_qkvg[0])
    key_part = projected[..., HD : 2 * HD].reshape(row_count, residues, HEADS, HEAD_DIM)
    values = projected[..., 2 * HD : 3 * HD].reshape(row_count, residues, HEADS, HEAD_DIM)
    bias_rows = jnp.einsum(
        "hc,ikc->hik", w_bias[0], normed, preferred_element_type=jnp.float32
    ).astype(jnp.bfloat16)
    proj_grid = projected.reshape(row_count, outer, span, 4 * HD)
    pair_grid = pair.reshape(row_count, outer, span, C)

    def start_block(bias_part, column, width):
        many = outer * width
        queries = lax.dynamic_slice_in_dim(proj_grid, column, width, 2).reshape(
            row_count, many, 4 * HD
        )
        query_part = queries[..., :HD].reshape(row_count, many, HEADS, HEAD_DIM)
        logits = jnp.einsum(
            "ijhd,ikhd->ihjk", query_part, key_part, preferred_element_type=jnp.float32
        )
        chain_here = lax.dynamic_slice_in_dim(chain_grid, column, width, 1).reshape(many)
        chain_cross = (chain_here[:, None] != chain[None, :]).astype(jnp.float32)
        bias_flat = jnp.transpose(bias_part, (1, 0, 2, 3)).reshape(HEADS, many, residues)
        logits = logits + bias_flat.astype(jnp.float32)[None]
        logits = logits + chain_offset[0][None, :, None, None] * chain_cross[None, None]
        logits = logits + key_mask
        weights = softmax_weights(logits)
        attended = jnp.einsum(
            "ihjk,ikhd->ijhd", weights, values, preferred_element_type=jnp.float32
        ).reshape(row_count, many, HD)
        gate_part = jax.nn.sigmoid(queries[..., 3 * HD :].astype(jnp.float32) + gate_bias[0])
        gated = (attended * gate_part).astype(jnp.bfloat16)
        update = (
            jnp.dot(gated.reshape(-1, HD), w_out[0], preferred_element_type=jnp.float32).reshape(
                row_count, many, C
            )
            + out_bias[0]
        )
        residual = lax.dynamic_slice_in_dim(pair_grid, column, width, 2).reshape(row_count, many, C)
        return (
            (residual.astype(jnp.float32) + update)
            .astype(jnp.bfloat16)
            .reshape(row_count, outer, width, C)
        )

    bias_outer = lax.all_gather(bias_rows[None], "row", axis=0, tiled=True)
    bias_piece = lax.all_gather(bias_outer, "sub", axis=2, tiled=True)
    piece_width = bias_piece.shape[2]
    step_width = math.gcd(piece_width, step_cap)
    block_count = piece_width // step_width

    def start_single(number):
        first_col = number * step_width
        bias_part = lax.dynamic_slice_in_dim(bias_piece, first_col, step_width, 2)
        return start_block(bias_part, first_col, step_width)

    results = lax.map(start_single, jnp.arange(block_count, dtype=jnp.int32))
    started_grid = jnp.transpose(results, (1, 2, 0, 3, 4)).reshape(row_count, outer, piece_width, C)
    started = started_grid.reshape(row_count, residues, C)
    columns = lax.all_to_all(started, ("row", "sub"), split_axis=1, concat_axis=0, tiled=True)
    col_count = columns.shape[1]
    normed_two = layer_norm(columns, ln_gain[1], ln_shift[1])
    projected_two = project(normed_two, w_qkvg[1])
    key_two = projected_two[..., HD : 2 * HD].reshape(residues, col_count, HEADS, HEAD_DIM)
    values_two = projected_two[..., 2 * HD : 3 * HD].reshape(residues, col_count, HEADS, HEAD_DIM)
    proj_two_grid = projected_two.reshape(outer, span, col_count, 4 * HD)
    column_grid = columns.reshape(outer, span, col_count, C)

    def end_block(bias_part, first_row, width):
        many = outer * width
        queries = lax.dynamic_slice_in_dim(proj_two_grid, first_row, width, 1).reshape(
            many, col_count, 4 * HD
        )
        query_part = queries[..., :HD].reshape(many, col_count, HEADS, HEAD_DIM)
        logits = jnp.einsum(
            "ijhd,kjhd->ijhk", query_part, key_two, preferred_element_type=jnp.float32
        )
        chain_here = lax.dynamic_slice_in_dim(chain_grid, first_row, width, 1).reshape(many)
        chain_cross = (chain_here[:, None] != chain[None, :]).astype(jnp.float32)
        bias_flat = jnp.transpose(bias_part, (0, 3, 1, 2)).reshape(many, HEADS, residues)
        logits = logits + bias_flat.astype(jnp.float32)[:, None]
        logits = logits + chain_offset[1][None, None, :, None] * chain_cross[:, None, None, :]
        logits = logits + key_mask
        weights = softmax_weights(logits)
        attended = jnp.einsum(
            "ijhk,kjhd->ijhd", weights, values_two, preferred_element_type=jnp.float32
        ).reshape(many, col_count, HD)
        gate_part = jax.nn.sigmoid(queries[..., 3 * HD :].astype(jnp.float32) + gate_bias[1])
        gated = (attended * gate_part).astype(jnp.bfloat16)
        update = (
            jnp.dot(gated.reshape(-1, HD), w_out[1], preferred_element_type=jnp.float32).reshape(
                many, col_count, C
            )
            + out_bias[1]
        )
        residual = lax.dynamic_slice_in_dim(column_grid, first_row, width, 1).reshape(
            many, col_count, C
        )
        return (
            (residual.astype(jnp.float32) + update)
            .astype(jnp.bfloat16)
            .reshape(outer, width, col_count, C)
        )

    bias_cols = jnp.einsum(
        "hc,kic->hki", w_bias[1], normed_two, preferred_element_type=jnp.float32
    ).astype(jnp.bfloat16)
    bias_outer_two = lax.all_gather(bias_cols[None], "row", axis=0, tiled=True)
    end_bias_piece = lax.all_gather(bias_outer_two, "sub", axis=3, tiled=True)
    piece_width = end_bias_piece.shape[3]
    end_step_width = math.gcd(piece_width, step_cap)
    block_count = piece_width // end_step_width

    def end_single(number):
        first_row = number * end_step_width
        bias_part = lax.dynamic_slice_in_dim(end_bias_piece, first_row, end_step_width, 3)
        return end_block(bias_part, first_row, end_step_width)

    results = lax.map(end_single, jnp.arange(block_count, dtype=jnp.int32))
    ended_grid = jnp.transpose(results, (1, 0, 2, 3, 4)).reshape(outer, piece_width, col_count, C)
    return ended_grid.reshape(residues, col_count, C)


def solution(mesh):
    in_specs = (
        P(("grp", "row", "sub"), None, None),
        P("grp"),
        P("grp"),
        P(),
        P(),
        P(),
        P(),
        P(),
        P(),
        P(),
        P(),
    )
    out_specs = P("grp", ("row", "sub"), None)
    return jax.shard_map(local, mesh=mesh, in_specs=in_specs, out_specs=out_specs, check_vma=False)
```

profile of v0, /device:TPU:0, one launch (start us, length us, event | category | flops | bytes accessed | tf_op | source)
XLA Modules:
  0.0 87.3 jit_solution(12496765934157148399)
XLA Ops:
  0.0 1.1 %convert_reduce_fusion.1 = f32[4,128]{1,0:T(4,128)S(1)} fusion(bf16[4,128,128]{2,1,0:T(8,128)(2,1)} %param.15), kind=kLoop, calls=%fused_computation.73 | loop fusion | flops 130560 | bytes 133120 | tf_op jit(solution)/shard_map/reduce_sum | solution.py:19
  3.0 10.5 %all-gather = bf16[32,4,128]{2,1,0:T(4,128)(2,1)S(1)} all-gather(bf16[4,4,128]{2,1,0:T(4,128)(2,1)S(1)} %copy.59), channel_id=2, replica_groups=mesh['grp'=1,'row'=8,'sub'=4] {'row'}, dimensions={0}, use_global_device_ids=true | all-gather | bytes 36864 | tf_op jit(solution)/shard_map/all_gather | solution.py:91
  13.6 13.7 %all_gather.13 = bf16[8,4,16,128]{3,0,1,2:T(8,128)(2,1)S(1)} all-gather(bf16[8,4,4,128]{3,0,1,2:T(8,128)(2,1)S(1)} %copy.60), channel_id=1, replica_groups=mesh['grp'=1,'row'=8,'sub'=4] {'sub'}, dimensions={2}, use_global_device_ids=true | all-gather | bytes 163840 | tf_op jit(solution)/shard_map/all_gather | solution.py:92
  27.4 0.6 copy-done.10
  28.0 0.7 copy-done.3
  28.6 9.9 %while.20 = (s32[]{:T(128)}, bf16[2,4,8,8,128]{4,3,0,2,1:T(8,128)(2,1)S(1)}, s32[2]{0:T(128)S(1)}, bf16[4,8,16,128]{3,2,1,0:T(8,128)(2,1)S(1)}, bf16[4,8,16,512]...) while((s32[]{:T(128)}, ...), condition=%wide.region_5.6_spmd, body=%wide.region_2.5_spmd.sunk | while | flops 35439876 | bytes 4175915 | solution.py:102
  28.6 0.7 dynamic_slice.53
  30.8 0.6 fusion.109
  31.4 1.8 %fusion.111 = f32[4,4,64,32]{2,3,1,0:T(8,128)S(1)} fusion(bf16[4,128,4,32]{1,3,2,0:T(8,128)(2,1)S(1)} %get-tuple-element.549, f32[4,4,64]{2,1,0:T(4,128)S(1)} %fusion.109, f32[4,4,64,128]{3,2,1,0:T(8,128)S(1)} %fusion.110), kind=kOutput, calls=%fused_computation.13.clone.1 | convolution fusion | flops 8782975 | bytes 790528 | tf_op jit(solution)/shard_map/while/body/eval_jaxpr/ihjk,ikhd->ijhd/dot_general | solution.py:73
  33.6 0.7 dynamic_slice.53
  35.8 0.6 fusion.109
  36.4 1.8 %fusion.111 = f32[4,4,64,32]{2,3,1,0:T(8,128)S(1)} fusion(bf16[4,128,4,32]{1,3,2,0:T(8,128)(2,1)S(1)} %get-tuple-element.549, f32[4,4,64]{2,1,0:T(4,128)S(1)} %fusion.109, f32[4,4,64,128]{3,2,1,0:T(8,128)S(1)} %fusion.110), kind=kOutput, calls=%fused_computation.13.clone.1 | convolution fusion | flops 8782975 | bytes 790528 | tf_op jit(solution)/shard_map/while/body/eval_jaxpr/ihjk,ikhd->ijhd/dot_general | solution.py:73
  38.6 0.8 copy.64
  39.3 4.8 %all-to-all-start = ((bf16[4,128,128]{2,0,1:T(4,128)(2,1)}), bf16[4,128,128]{2,0,1:T(4,128)(2,1)S(1)}, u32[]{:S(2)}, u32[]{:S(2)}) async-start(bf16[4,128,128]{2,0,1:T(4,128)(2,1)} %copy.64), calls=%async_computation | async-start | bytes 262144 | tf_op jit(solution)/shard_map/all_to_all | solution.py:105
  44.1 8.4 %all-to-all-done = bf16[4,128,128]{2,0,1:T(4,128)(2,1)S(1)} async-done(((bf16[4,128,128]{2,0,1:T(4,128)(2,1)}), bf16[4,128,128]{2,0,1:T(4,128)(2,1)S(1)}, u32[]{:S(2)}, u32[]{:S(2)}) %all-to-all-start) | async-done | bytes 131104 | tf_op jit(solution)/shard_map/all_to_all | solution.py:105
  54.9 8.3 %all-gather.1 = bf16[32,128,4]{1,2,0:T(4,128)(2,1)S(1)} all-gather(bf16[4,128,4]{1,2,0:T(4,128)(2,1)S(1)} %copy.70), channel_id=3, replica_groups=mesh['grp'=1,'row'=8,'sub'=4] {'row'}, dimensions={0}, use_global_device_ids=true | all-gather | bytes 36864 | tf_op jit(solution)/shard_map/all_gather | solution.py:153
  63.2 13.4 %all_gather.15 = bf16[8,4,128,16]{2,0,1,3:T(8,128)(2,1)S(1)} all-gather(bf16[8,4,128,4]{2,0,1,3:T(8,128)(2,1)S(1)} %copy.71), channel_id=1, replica_groups=mesh['grp'=1,'row'=8,'sub'=4] {'sub'}, dimensions={3}, use_global_device_ids=true | all-gather | bytes 163840 | tf_op jit(solution)/shard_map/all_gather | solution.py:154
  76.6 9.9 %while.21 = (s32[]{:T(128)}, bf16[2,8,8,4,128]{4,2,1,3,0:T(8,128)(2,1)S(1)}, s32[2]{0:T(128)S(1)}, bf16[8,16,4,128]{3,1,0,2:T(8,128)(2,1)S(1)}, bf16[8,16,4,512]...) while((s32[]{:T(128)}, ...), condition=%wide.region_11.12_spmd, body=%wide.region_8.11_spmd.sunk | while | flops 35439876 | bytes 4700203 | solution.py:164
  76.6 0.6 dynamic_slice.58
  78.8 0.6 fusion.120
  79.4 1.8 %fusion.122 = f32[4,4,64,32]{2,3,1,0:T(8,128)S(1)} fusion(bf16[128,4,4,32]{0,3,2,1:T(8,128)(2,1)S(1)} %get-tuple-element.606, f32[64,4,4]{0,2,1:T(4,128)S(1)} %fusion.120, f32[64,4,4,128]{3,0,2,1:T(8,128)S(1)} %fusion.121), kind=kOutput, calls=%fused_computation.44.clone.1 | convolution fusion | flops 8782975 | bytes 790528 | tf_op jit(solution)/shard_map/while/body/eval_jaxpr/ijhk,kjhd->ijhd/dot_general | solution.py:130
  81.5 0.6 dynamic_slice.58
  84.3 1.8 %fusion.122 = f32[4,4,64,32]{2,3,1,0:T(8,128)S(1)} fusion(bf16[128,4,4,32]{0,3,2,1:T(8,128)(2,1)S(1)} %get-tuple-element.606, f32[64,4,4]{0,2,1:T(4,128)S(1)} %fusion.120, f32[64,4,4,128]{3,0,2,1:T(8,128)S(1)} %fusion.121), kind=kOutput, calls=%fused_computation.44.clone.1 | convolution fusion | flops 8782975 | bytes 790528 | tf_op jit(solution)/shard_map/while/body/eval_jaxpr/ijhk,kjhd->ijhd/dot_general | solution.py:130
  86.5 0.8 copy.75
  (116 shorter events, 9.4 us)
Async XLA Ops:
  0.0 1.1 %copy-start = (bf16[4,128,128]{2,1,0:T(8,128)(2,1)S(1)}, bf16[4,128,128]{2,1,0:T(8,128)(2,1)}, u32[]{:S(2)}) copy-start(bf16[4,128,128]{2,1,0:T(8,128)(2,1)} %param.15) | copy-start | bytes 393220
  0.0 1.4 %copy-start.6 = (f32[2,128]{1,0:T(2,128)S(1)}, f32[2,128]{1,0:T(2,128)}, u32[]{:S(2)}) copy-start(f32[2,128]{1,0:T(2,128)} %param.19) | copy-start | bytes 3076
  0.0 1.4 %copy-start.7 = (f32[2,128]{1,0:T(2,128)S(1)}, f32[2,128]{1,0:T(2,128)}, u32[]{:S(2)}) copy-start(f32[2,128]{1,0:T(2,128)} %param.18) | copy-start | bytes 3076
  0.0 1.6 %copy-start.1 = (bf16[2,128,512]{2,1,0:T(8,128)(2,1)S(1)}, bf16[2,128,512]{2,1,0:T(8,128)(2,1)}, u32[]{:S(2)}) copy-start(bf16[2,128,512]{2,1,0:T(8,128)(2,1)} %param.20) | copy-start | bytes 786436
  2.1 0.7 copy-start.5
  13.5 13.8 %copy-start.2 = (s32[128]{0:T(128)S(1)}, s32[128]{0:T(128)}, u32[]{:S(2)}) copy-start(s32[128]{0:T(128)} %param.17) | copy-start | bytes 1540
  13.5 14.4 %copy-start.4 = (f32[2,128]{1,0:T(2,128)S(1)}, f32[2,128]{1,0:T(2,128)}, u32[]{:S(2)}) copy-start(f32[2,128]{1,0:T(2,128)} %param.24) | copy-start | bytes 3076
  13.5 14.4 %copy-start.8 = (bf16[2,128,128]{2,1,0:T(8,128)(2,1)S(1)}, bf16[2,128,128]{2,1,0:T(8,128)(2,1)}, u32[]{:S(2)}) copy-start(bf16[2,128,128]{2,1,0:T(8,128)(2,1)} %param.23) | copy-start | bytes 196612
  13.5 14.4 %copy-start.9 = (f32[2,4]{1,0:T(2,128)S(1)}, f32[2,4]{1,0:T(2,128)}, u32[]{:S(2)}) copy-start(f32[2,4]{1,0:T(2,128)} %param.25) | copy-start | bytes 100
  27.3 0.7 copy-start.10
  27.9 0.7 copy-start.3
  39.3 13.2 %all-to-all-start = ((bf16[4,128,128]{2,0,1:T(4,128)(2,1)}), bf16[4,128,128]{2,0,1:T(4,128)(2,1)S(1)}, u32[]{:S(2)}, u32[]{:S(2)}) async-start(bf16[4,128,128]{2,0,1:T(4,128)(2,1)} %copy.64), calls=%async_computation | async-start | bytes 262144 | tf_op jit(solution)/shard_map/all_to_all | solution.py:105
where the time goes:
time: 87.6 us; the launch traced here: 87.3 us
  blocking collectives  46 us (53%)
  matrix products  12.3 us (14%)
  local copies, waits for them, and re-layouts  9.29 us (11%)
  waiting for transfers between devices  8.39 us (10%)
  starting transfers between devices  4.75 us (5%)
  other arithmetic  3.23 us (4%)
  loops' own time  3.1 us (4%)
    all_gather x1, blocking collectives, local(): bias_piece = lax.all_gather(bias_outer, 'sub', axis=2, tiled=True)  13.7 us
    all_gather x1, blocking collectives, local(): end_bias_piece = lax.all_gather(bias_outer_two, 'sub', axis=3, tiled=True)  13.4 us
    all_gather x1, blocking collectives, local(): bias_outer = lax.all_gather(bias_rows[None], 'row', axis=0, tiled=True)  10.5 us
    all_to_all x1, waiting for transfers between devices, local(): lax.all_to_all(started, ('row', 'sub'), split_axis=1, concat_axis=0, tile...  8.39 us
    all_gather x1, blocking collectives, local(): bias_outer_two = lax.all_gather(bias_cols[None], 'row', axis=0, tiled=True)  8.34 us
    all_to_all x1, starting transfers between devices, local(): lax.all_to_all(started, ('row', 'sub'), split_axis=1, concat_axis=0, tile...  4.75 us
    dot_general x2, matrix products, start_block(): jnp.einsum('ihjk,ikhd->ijhd', weights, values, preferred_element_type=jnp...  3.69 us
    dot_general x2, matrix products, end_block(): jnp.einsum('ijhk,kjhd->ijhd', weights, values_two, preferred_element_type...  3.69 us
  transfers between devices with their start and end apart: 1, of which 1 were waited for; matrix products, arithmetic and copies ran while one was open for 0% of the time, Pallas kernels for 0%

commit v1 on v0

v1 whole, which is shorter than its diff:
```python
import functools

import jax
import jax.numpy as jnp
from jax import lax
from jax.experimental import pallas as pl
from jax.experimental.pallas import tpu as pltpu
from jax.sharding import PartitionSpec as P

C = 128
HEADS = 4
HEAD_DIM = 32
HD = 128
LANES = 128
EPS = 1e-05

F32 = jnp.float32
BF16 = jnp.bfloat16
NN = (((1,), (0,)), ((), ()))
NT = (((1,), (1,)), ((), ()))


def matmul(a, b, dims=NN):
    return lax.dot_general(a, b, dims, preferred_element_type=F32)


def layer_norm(values, gain_row, shift_row):
    middle = jnp.mean(values, axis=-1, keepdims=True)
    centred = values - middle
    spread = jnp.mean(jnp.square(centred), axis=-1, keepdims=True)
    return (centred * lax.rsqrt(spread + EPS) * gain_row + shift_row).astype(BF16)


def head_mask(head):
    lane = lax.broadcasted_iota(jnp.int32, (1, HD), 1)
    return jnp.where(lane // HEAD_DIM == head, 1.0, 0.0).astype(F32)


def each(count, unrolled, body):
    if unrolled:
        for index in range(count):
            body(index)
    else:
        lax.fori_loop(0, count, lambda index, _: (body(index), 0)[1], 0)


def column_of(row):
    n = row.shape[1]
    first = lax.broadcasted_iota(jnp.int32, (n, n), 0)
    second = lax.broadcasted_iota(jnp.int32, (n, n), 1)
    return jnp.sum(jnp.where(first == second, row, 0.0), axis=1, keepdims=True)


def fill_bias(layer, flip, received, wide, total, mask, chain, chain_offset):
    n = total.shape[1]
    parts, slots = received.shape[0], wide.shape[0] // received.shape[0]
    chain_row = chain[...].astype(F32)
    chain_column = column_of(chain_row)
    key_row = jnp.where(mask[...] > 0, 0.0, -1000000000.0).astype(F32)
    for tile in range(n // LANES):
        block = received[:, tile * slots : (tile + 1) * slots, :].astype(F32)
        wide[...] = block.reshape(parts * slots, LANES)
        span = slice(tile * LANES, (tile + 1) * LANES)
        cross = (chain_column[span] if flip else chain_column) != (
            chain_row if flip else chain_row[:, span]
        )
        for head in range(HEADS):
            known = jnp.where(cross, chain_offset[layer, head], 0.0)
            known = known + (key_row if flip else key_row[:, span])
            gathered = wide[pl.ds(head, n, stride=HEADS), :]
            if flip:
                first = head * n + tile * LANES
                total[first : first + LANES, :] = gathered.T + known
            else:
                total[head * n : (head + 1) * n, span] = gathered + known


def attend(normed, entries, layer, total, w_qkvg, gate_bias, w_out, out_bias):
    n = normed.shape[0]
    projected = matmul(normed, w_qkvg[layer])
    queries = projected[:, :HD] * (HEAD_DIM ** (-0.5))
    keys = projected[:, HD : 2 * HD].astype(BF16)
    values = projected[:, 2 * HD : 3 * HD]
    gates = projected[:, 3 * HD :].astype(BF16).astype(F32)
    attended = jnp.zeros((n, HD), F32)
    for head in range(HEADS):
        own = head_mask(head)
        logits = matmul((queries * own).astype(BF16), keys, NT)
        logits = logits + total[head * n : (head + 1) * n, :]
        expon = jnp.exp(logits - jnp.max(logits, axis=-1, keepdims=True))
        weights = (expon / jnp.sum(expon, axis=-1, keepdims=True)).astype(BF16)
        attended = attended + matmul(weights, (values * own).astype(BF16))
    gated = (attended * jax.nn.sigmoid(gates + gate_bias[layer : layer + 1, :])).astype(BF16)
    update = matmul(gated, w_out[layer]) + out_bias[layer : layer + 1, :]
    return (entries + update).astype(BF16)


def bias_rows(normed, w_bias, layer):
    return matmul(w_bias[layer], normed, NT)


def first_kernel(pair, ln_gain, ln_shift, w_bias, out, narrow):
    parts, n = out.shape[0], narrow.shape[1]
    rows, slots = pair.shape[0] // n, narrow.shape[0]
    for row in range(rows):
        entries = pair[row * n : (row + 1) * n, :].astype(F32)
        normed = layer_norm(entries, ln_gain[0:1, :], ln_shift[0:1, :])
        narrow[row * HEADS : (row + 1) * HEADS, :] = bias_rows(normed, w_bias, 0)
    for tile in range(n // LANES):
        block = narrow[:, tile * LANES : (tile + 1) * LANES].astype(BF16)
        out[:, tile * slots : (tile + 1) * slots, :] = jnp.broadcast_to(
            block[None], (parts, slots, LANES)
        )


def start_kernel(
    chain_offset, received, pair, mask, chain, ln_gain, ln_shift, w_qkvg, gate_bias, w_bias, w_out,
    out_bias, out, wide, total, narrow, column, packed, apart,
):
    parts, n = out.shape[0], total.shape[1]
    rows, slots = pair.shape[0] // n, narrow.shape[0]
    square = rows * rows
    fill_bias(0, False, received, wide, total, mask, chain, chain_offset)

    def row_step(row):
        here = pl.ds(pl.multiple_of(row * n, LANES), n)
        entries = pair[here, :].astype(F32)
        normed = layer_norm(entries, ln_gain[0:1, :], ln_shift[0:1, :])
        started = attend(normed, entries, 0, total, w_qkvg, gate_bias, w_out, out_bias).astype(F32)
        column[...] = started
        for place in range(rows):
            packed[pl.ds(row * rows + place, parts, stride=square), :] = column[
                pl.ds(place, parts, stride=rows), :
            ]
        normed = layer_norm(started, ln_gain[1:2, :], ln_shift[1:2, :])
        apart[row, :, :] = bias_rows(normed, w_bias, 1)

    each(rows, n <= LANES, row_step)
    for row in range(rows):
        narrow[row * HEADS : (row + 1) * HEADS, :] = apart[row, :, :]
    out[:, :square, :] = packed[...].reshape(parts, square, LANES).astype(BF16)
    for tile in range(n // LANES):
        block = narrow[:, tile * LANES : (tile + 1) * LANES].astype(BF16)
        first = square + tile * slots
        out[:, first : first + slots, :] = jnp.broadcast_to(block[None], (parts, slots, LANES))


def end_kernel(
    chain_offset, received, mask, chain, ln_gain, ln_shift, w_qkvg, gate_bias, w_out, out_bias, out,
    wide, total, packed, column,
):
    parts, n = received.shape[0], total.shape[1]
    rows = packed.shape[0] // n
    square = rows * rows
    fill_bias(
        1, True, received.at[:, square:, :], wide, total, mask, chain, chain_offset
    )
    packed[...] = received[:, :square, :].astype(F32).reshape(parts * square, LANES)

    def column_step(place):
        here = pl.ds(place, n, stride=rows)
        entries = packed[here, :]
        normed = layer_norm(entries, ln_gain[1:2, :], ln_shift[1:2, :])
        ended = attend(normed, entries, 1, total, w_qkvg, gate_bias, w_out, out_bias)
        packed[here, :] = ended.astype(F32)

    each(rows, n <= LANES, column_step)
    out[...] = packed[...].astype(BF16)


def call(kernel, out_shape, scratch, operands, scalars=1):
    specs = [pl.BlockSpec(memory_space=pltpu.SMEM)] * scalars
    specs += [pl.BlockSpec(memory_space=pltpu.VMEM)] * (len(operands) - scalars)
    return pl.pallas_call(
        kernel,
        out_shape=out_shape,
        in_specs=specs,
        out_specs=pl.BlockSpec(memory_space=pltpu.VMEM),
        scratch_shapes=scratch,
        compiler_params=pltpu.CompilerParams(vmem_limit_bytes=40 * 1024 * 1024),
    )(*operands)


def local(
    pair, mask, chain, ln_gain, ln_shift, w_qkvg, gate_bias, w_bias, w_out, out_bias, chain_offset
):
    rows, n = pair.shape[0], pair.shape[1]
    parts = lax.axis_size("row") * lax.axis_size("sub")
    tiles, slots, square = n // LANES, rows * HEADS, rows * rows
    exchange = functools.partial(
        lax.all_to_all, axis_name=("row", "sub"), split_axis=0, concat_axis=0, tiled=True
    )
    flat = pair.reshape(rows * n, C)
    mask_row, chain_row = mask.reshape(1, n), chain.reshape(1, n)
    shared = [
        pltpu.VMEM((parts * slots, LANES), F32),
        pltpu.VMEM((HEADS * n, n), F32),
    ]
    bias_part = call(
        first_kernel,
        jax.ShapeDtypeStruct((parts, tiles * slots, LANES), BF16),
        [pltpu.VMEM((slots, n), F32)],
        (flat, ln_gain, ln_shift, w_bias),
        scalars=0,
    )
    bias_all = exchange(bias_part)
    sent = call(
        start_kernel,
        jax.ShapeDtypeStruct((parts, square + tiles * slots, LANES), BF16),
        shared
        + [
            pltpu.VMEM((slots, n), F32),
            pltpu.VMEM((n, C), F32),
            pltpu.VMEM((rows * n, C), F32),
            pltpu.VMEM((rows, HEADS, n), F32),
        ],
        (
            chain_offset, bias_all, flat, mask_row, chain_row, ln_gain, ln_shift, w_qkvg, gate_bias,
            w_bias, w_out, out_bias,
        ),
    )
    columns = exchange(sent)
    ended = call(
        end_kernel,
        jax.ShapeDtypeStruct((n * rows, C), BF16),
        shared + [pltpu.VMEM((rows * n, C), F32), pltpu.VMEM((n, C), F32)],
        (
            chain_offset, columns, mask_row, chain_row, ln_gain, ln_shift, w_qkvg, gate_bias, w_out,
            out_bias,
        ),
    )
    return ended.reshape(n, rows, C)


def solution(mesh):
    in_specs = (
        P(("grp", "row", "sub"), None, None),
        P("grp"),
        P("grp"),
        P(),
        P(),
        P(),
        P(),
        P(),
        P(),
        P(),
        P(),
    )
    out_specs = P("grp", ("row", "sub"), None)
    return jax.shard_map(local, mesh=mesh, in_specs=in_specs, out_specs=out_specs, check_vma=False)
```

time: 87.6 us -> 41.1 us (0.47)
  blocking collectives: 46 us -> 27.4 us
  matrix products: 12.3 us -> 0 us
  Pallas kernels: 0 us -> 9.72 us
  waiting for transfers between devices: 8.39 us -> 0 us
  local copies, waits for them, and re-layouts: 9.29 us -> 3.62 us
  starting transfers between devices: 4.75 us -> 0 us
  other arithmetic: 3.23 us -> 0 us
  loops' own time: 3.1 us -> 0 us
    all_gather x4 -> x0, blocking collectives: 46 us -> none  [the longest x1 13.7 us: local(): bias_piece = lax.all_gather(bias_outer, 'sub', axis=2, tiled=True)]
    all_to_all x0 -> x2, blocking collectives: none -> 27.4 us  [the longest x1 15.5 us: local(): bias_all = exchange(bias_part)]
    dot_general x16 -> x0, matrix products: 10 us -> none  [the longest x2 3.69 us: start_block(): jnp.einsum('ihjk,ikhd->ijhd', weights, values, preferred_element_type=jnp...]
    pallas_call x0 -> x3, Pallas kernels: none -> 9.72 us  [call(): pl.pallas_call(kernel, out_shape=out_shape, in_specs=specs, out_specs=pl....]
    all_to_all x1 -> x0, waiting for transfers between devices: 8.39 us -> none  [local(): lax.all_to_all(started, ('row', 'sub'), split_axis=1, concat_axis=0, tile...]
    all_to_all x1 -> x0, starting transfers between devices: 4.75 us -> none  [local(): lax.all_to_all(started, ('row', 'sub'), split_axis=1, concat_axis=0, tile...]
    dynamic_slice x16 -> x0, local copies, waits for them, and re-layouts: 3.15 us -> none  [the longest x4 2.5 us: local(): results = lax.map(start_single, jnp.arange(block_count, dtype=jnp.int32))]
    another operation x2 -> x0, loops' own time: 3.1 us -> none  [the longest x1 1.59 us: local(): results = lax.map(start_single, jnp.arange(block_count, dtype=jnp.int32))]
  transfers between devices with their start and end apart: 1 -> 0, of which waited for: 1 -> 0; matrix products, arithmetic and copies ran while one was open for 0% -> 0% of each run, Pallas kernels for 0% -> 0%
where the time goes in v1:
time: 41.1 us; the launch traced here: 40.8 us
  blocking collectives  27.4 us (67%)
  Pallas kernels  9.72 us (24%)
  local copies, waits for them, and re-layouts  3.62 us (9%)
    all_to_all x1, blocking collectives, local(): bias_all = exchange(bias_part)  15.5 us
    all_to_all x1, blocking collectives, local(): columns = exchange(sent)  11.9 us
    pallas_call x3, Pallas kernels, call(): pl.pallas_call(kernel, out_shape=out_shape, in_specs=specs, out_specs=pl....  9.72 us
    unnamed x24, local copies, waits for them, and re-layouts  3.62 us

profile of v1, /device:TPU:0, one launch (start us, length us, event | category | flops | bytes accessed | tf_op | source)
XLA Modules:
  0.0 40.8 jit_solution(731439328513823739)
XLA Ops:
  0.0 0.0 copy-start.3
  0.0 0.7 %copy-done.3 = f32[2,128]{1,0:T(2,128)S(1)} copy-done((f32[2,128]{1,0:T(2,128)S(1)}, f32[2,128]{1,0:T(2,128)}, u32[]{:S(2)}) %copy-start.3) | copy-done | bytes 1048
  0.7 0.0 copy-start.1
  0.7 0.9 %copy-done.1 = bf16[4,128,128]{2,1,0:T(8,128)(2,1)S(1)} copy-done((bf16[4,128,128]{2,1,0:T(8,128)(2,1)S(1)}, bf16[4,128,128]{2,1,0:T(8,128)(2,1)}, u32[]{:S(2)}) %copy-start.1) | copy-done | bytes 131096
  1.6 0.7 %copy-done.4 = f32[2,128]{1,0:T(2,128)S(1)} copy-done((f32[2,128]{1,0:T(2,128)S(1)}, f32[2,128]{1,0:T(2,128)}, u32[]{:S(2)}) %copy-start.4) | copy-done | bytes 1048
  2.3 0.7 %copy-done.6 = bf16[2,4,128]{2,1,0:T(4,128)(2,1)S(1)} copy-done((bf16[2,4,128]{2,1,0:T(4,128)(2,1)S(1)}, bf16[2,4,128]{2,1,0:T(4,128)(2,1)}, u32[]{:S(2)}) %copy-start.6) | copy-done | bytes 2072
  2.9 0.4 shard_map.109
  3.4 0.0 copy-start.2
  3.4 0.0 copy-start.8
  3.4 0.0 copy-start.9
  3.4 0.0 copy-start.11
  3.4 15.5 %all_to_all.10.received = bf16[32,16,128]{2,1,0:T(8,128)(2,1)S(1)} all-to-all(bf16[32,16,128]{2,1,0:T(8,128)(2,1)S(1)} %shard_map.109), channel_id=1, replica_groups=mesh['grp'=1,'row'=8,'sub'=4] {'row','sub'}, dimensions={0} | all-to-all | bytes 262144 | tf_op jit(solution)/shard_map/all_to_all | solution.py:206
  18.9 0.0 copy-done
  18.9 0.0 copy-done.2
  18.9 0.0 copy-done.8
  18.9 0.0 copy-done.9
  18.9 0.0 copy-done.11
  19.0 0.6 %copy-done.7 = f32[2,4]{1,0:T(2,128)S(1)} copy-done((f32[2,4]{1,0:T(2,128)S(1)}, f32[2,4]{1,0:T(2,128)}, u32[]{:S(2)}) %copy-start.7) | copy-done | bytes 56
  19.6 0.0 copy-done.10
  19.6 5.2 %shard_map.110 = bf16[32,32,128]{2,1,0:T(8,128)(2,1)S(1)} custom-call(f32[2,4]{1,0:T(2,128)S(1)} %copy-done.7, bf16[32,16,128]{2,1,0:T(8,128)(2,1)S(1)} %all_to_all.10.received, bf16[512,128]{1,0:T(8,128)(2,1)S(1)} %bitcast.5, s32[1,128]{1,0:T(1,128)S(1)} %bitcast.6, s32[1,128]{1,0:T(1,128)S(1)} %bitcast.8, f32[2,128]{1,0:T(2,128)S(1)} %copy-done.3, ...), custom_call_target="tpu_custom_call" | custom-call | tf_op jit(solution)/shard_map/pallas_call | solution.py:174
  24.8 0.0 copy-start.5
  24.8 11.9 %all_to_all.11.received = bf16[32,32,128]{2,1,0:T(8,128)(2,1)S(1)} all-to-all(bf16[32,32,128]{2,1,0:T(8,128)(2,1)S(1)} %shard_map.110), channel_id=1, replica_groups=mesh['grp'=1,'row'=8,'sub'=4] {'row','sub'}, dimensions={0} | all-to-all | bytes 524288 | tf_op jit(solution)/shard_map/all_to_all | solution.py:222
  36.7 0.0 copy-done.5
  36.7 4.2 %shard_map.111 = bf16[512,128]{1,0:T(8,128)(2,1)} custom-call(f32[2,4]{1,0:T(2,128)S(1)} %copy-done.7, bf16[32,32,128]{2,1,0:T(8,128)(2,1)S(1)} %all_to_all.11.received, s32[1,128]{1,0:T(1,128)S(1)} %bitcast.7, s32[1,128]{1,0:T(1,128)S(1)} %bitcast.9, f32[2,128]{1,0:T(2,128)S(1)} %copy-done.3, f32[2,128]{1,0:T(2,128)S(1)} %copy-done.5, ...), custom_call_target="tpu_custom_call" | custom-call | tf_op jit(solution)/shard_map/pallas_call | solution.py:174
  (5 shorter events, 0.0 us)
Async XLA Ops:
  0.0 0.7 %copy-start.3 = (f32[2,128]{1,0:T(2,128)S(1)}, f32[2,128]{1,0:T(2,128)}, u32[]{:S(2)}) copy-start(f32[2,128]{1,0:T(2,128)} %ln_gain.5) | copy-start | bytes 3076
  0.7 0.9 %copy-start.1 = (bf16[4,128,128]{2,1,0:T(8,128)(2,1)S(1)}, bf16[4,128,128]{2,1,0:T(8,128)(2,1)}, u32[]{:S(2)}) copy-start(bf16[4,128,128]{2,1,0:T(8,128)(2,1)} %param.11) | copy-start | bytes 393220
  1.6 0.7 %copy-start.4 = (f32[2,128]{1,0:T(2,128)S(1)}, f32[2,128]{1,0:T(2,128)}, u32[]{:S(2)}) copy-start(f32[2,128]{1,0:T(2,128)} %ln_shift.5) | copy-start | bytes 3076
  2.3 0.7 %copy-start.6 = (bf16[2,4,128]{2,1,0:T(4,128)(2,1)S(1)}, bf16[2,4,128]{2,1,0:T(4,128)(2,1)}, u32[]{:S(2)}) copy-start(bf16[2,4,128]{2,1,0:T(4,128)(2,1)} %w_bias.3) | copy-start | bytes 6148
  2.9 16.0 %copy-start = (bf16[2,128,512]{2,1,0:T(8,128)(2,1)S(1)}, bf16[2,128,512]{2,1,0:T(8,128)(2,1)}, u32[]{:S(2)}) copy-start(bf16[2,128,512]{2,1,0:T(8,128)(2,1)} %w_qkvg.3) | copy-start | bytes 786436
  3.4 15.6 %copy-start.2 = (bf16[2,128,128]{2,1,0:T(8,128)(2,1)S(1)}, bf16[2,128,128]{2,1,0:T(8,128)(2,1)}, u32[]{:S(2)}) copy-start(bf16[2,128,128]{2,1,0:T(8,128)(2,1)} %w_out.3) | copy-start | bytes 196612
  3.4 15.6 %copy-start.8 = (f32[2,128]{1,0:T(2,128)S(1)}, f32[2,128]{1,0:T(2,128)}, u32[]{:S(2)}) copy-start(f32[2,128]{1,0:T(2,128)} %gate_bias.3) | copy-start | bytes 3076
  3.4 15.6 %copy-start.9 = (f32[2,128]{1,0:T(2,128)S(1)}, f32[2,128]{1,0:T(2,128)}, u32[]{:S(2)}) copy-start(f32[2,128]{1,0:T(2,128)} %out_bias.3) | copy-start | bytes 3076
  3.4 15.6 %copy-start.11 = (s32[128]{0:T(128)S(1)}, s32[128]{0:T(128)}, u32[]{:S(2)}) copy-start(s32[128]{0:T(128)} %param.13) | copy-start | bytes 1540
  18.9 0.7 %copy-start.7 = (f32[2,4]{1,0:T(2,128)S(1)}, f32[2,4]{1,0:T(2,128)}, u32[]{:S(2)}) copy-start(f32[2,4]{1,0:T(2,128)} %chain_offset.3) | copy-start | bytes 100
  18.9 0.7 %copy-start.10 = (s32[128]{0:T(128)S(1)}, s32[128]{0:T(128)}, u32[]{:S(2)}) copy-start(s32[128]{0:T(128)} %param.12) | copy-start | bytes 1540
  24.8 11.9 %copy-start.5 = (f32[2,128]{1,0:T(2,128)S(1)}, f32[2,128]{1,0:T(2,128)}, u32[]{:S(2)}) copy-start(f32[2,128]{1,0:T(2,128)} %ln_shift.5) | copy-start | bytes 3076

commit v2 on v1

v2 whole, which is shorter than its diff:
```python
import functools

import jax
import jax.numpy as jnp
from jax import lax
from jax.experimental import pallas as pl
from jax.experimental.pallas import tpu as pltpu
from jax.sharding import PartitionSpec as P

C = 128
HEADS = 4
HEAD_DIM = 32
HD = 128
LANES = 128
EPS = 1e-05

F32 = jnp.float32
BF16 = jnp.bfloat16
NN = (((1,), (0,)), ((), ()))
NT = (((1,), (1,)), ((), ()))


def matmul(a, b, dims=NN):
    return lax.dot_general(a, b, dims, preferred_element_type=F32)


def layer_norm(values, gain_row, shift_row):
    middle = jnp.mean(values, axis=-1, keepdims=True)
    centred = values - middle
    spread = jnp.mean(jnp.square(centred), axis=-1, keepdims=True)
    return (centred * lax.rsqrt(spread + EPS) * gain_row + shift_row).astype(BF16)


def head_mask(head):
    lane = lax.broadcasted_iota(jnp.int32, (1, HD), 1)
    return jnp.where(lane // HEAD_DIM == head, 1.0, 0.0).astype(F32)


def each(count, unrolled, body):
    if unrolled:
        for index in range(count):
            body(index)
    else:
        lax.fori_loop(0, count, lambda index, _: (body(index), 0)[1], 0)


def block(index, size):
    if isinstance(index, int):
        return slice(index * size, (index + 1) * size)
    return pl.ds(pl.multiple_of(index * size, size), size)


def column_of(row):
    n = row.shape[1]
    first = lax.broadcasted_iota(jnp.int32, (n, n), 0)
    second = lax.broadcasted_iota(jnp.int32, (n, n), 1)
    return jnp.sum(jnp.where(first == second, row, 0.0), axis=1, keepdims=True)


def known_logits(layer, mask, chain, chain_offset, total):
    n = total.shape[1]
    chain_row = chain[...].astype(F32)
    key_row = jnp.where(mask[...] > 0, 0.0, -1000000000.0).astype(F32)
    cross = column_of(chain_row) != chain_row
    for head in range(HEADS):
        total[block(head, n), :] = jnp.where(cross, chain_offset[layer, head], 0.0) + key_row


def add_bias(flip, received, first_slot, wide, known, total):
    n = total.shape[1]
    parts, slots = received.shape[0], wide.shape[0] // received.shape[0]
    for tile in range(n // LANES):
        first = first_slot + tile * slots
        wide[...] = received[:, first : first + slots, :].astype(F32).reshape(parts * slots, LANES)
        span = block(tile, LANES)
        for head in range(HEADS):
            gathered = wide[pl.ds(head, n, stride=HEADS), :]
            if flip:
                here = block(head * (n // LANES) + tile, LANES)
                total[here, :] = gathered.T + known[here, :]
            else:
                here = block(head, n)
                total[here, span] = gathered + known[here, span]


def project(normed, weights, gate_row, queries, keys, values, gates):
    n = normed.shape[0]
    projected = matmul(normed, weights)
    scaled = projected[:, :HD] * (HEAD_DIM ** (-0.5))
    keys[...] = projected[:, HD : 2 * HD].astype(BF16)
    held = projected[:, 2 * HD : 3 * HD]
    gates[...] = jax.nn.sigmoid(projected[:, 3 * HD :].astype(BF16).astype(F32) + gate_row)
    for head in range(HEADS):
        own = head_mask(head)
        queries[block(head, n), :] = (scaled * own).astype(BF16)
        values[block(head, n), :HD] = (held * own).astype(BF16)
        values[block(head, n), HD:] = jnp.broadcast_to(own.astype(BF16), (n, HD))


def attend(queries, keys, values, gates, total, w_out, out_row):
    n = keys.shape[0]
    logits = matmul(queries[...], keys[...], NT) + total[...]
    expon = jnp.exp(logits - jnp.max(logits, axis=-1, keepdims=True)).astype(BF16)
    beside = jnp.concatenate([expon[block(head, n), :] for head in range(HEADS)], axis=1)
    summed = matmul(beside, values[...])
    gated = (summed[:, :HD] / summed[:, HD:] * gates[...]).astype(BF16)
    return matmul(gated, w_out) + out_row


def bias_rows(normed, w_bias, layer):
    return matmul(w_bias[layer], normed, NT)


def pack_bias(narrow, first_slot, out):
    parts, (slots, n) = out.shape[0], narrow.shape
    for tile in range(n // LANES):
        part = narrow[:, block(tile, LANES)].astype(BF16)
        first = first_slot + tile * slots
        out[:, first : first + slots, :] = jnp.broadcast_to(part[None], (parts, slots, LANES))


def fetch(pairs, sems):
    copies = [
        pltpu.make_async_copy(far, near, sems.at[index]) for index, (far, near) in enumerate(pairs)
    ]
    for copy in copies:
        copy.start()
    return copies


def bias_kernel(
    pair_far, gain_far, shift_far, bias_far, out, normed_out, pair, ln_gain, ln_shift, w_bias, narrow, sems
):
    n = narrow.shape[1]
    far, near = (pair_far, gain_far, shift_far, bias_far), (pair, ln_gain, ln_shift, w_bias)
    for copy in fetch(zip(far, near, strict=True), sems):
        copy.wait()
    for row in range(pair.shape[0] // n):
        entries = pair[block(row, n), :].astype(F32)
        normed = layer_norm(entries, ln_gain[0:1, :], ln_shift[0:1, :])
        normed_out[block(row, n), :] = normed
        narrow[block(row, HEADS), :] = bias_rows(normed, w_bias, 0)
    pack_bias(narrow, 0, out)


def project_kernel(
    offset_far, mask_far, chain_far, w_far, gate_far, w_out_far, out_bias_far, normed,
    queries, keys, values, gates, known_start, known_end, w_qkvg, gate_bias, w_out, out_bias,
    chain_offset, mask, chain, sems,
):
    n = known_start.shape[1]
    far = (w_far, gate_far, offset_far, mask_far, chain_far, w_out_far, out_bias_far)
    near = (w_qkvg, gate_bias, chain_offset, mask, chain, w_out, out_bias)
    copies = fetch(zip(far, near, strict=True), sems)
    copies[0].wait()
    copies[1].wait()

    def row_step(row):
        here, wide = block(row, n), block(row, HEADS * n)
        project(
            normed[here, :], w_qkvg[0], gate_bias[0:1, :], queries.at[wide, :], keys.at[here, :],
            values.at[wide, :], gates.at[here, :],
        )

    each(keys.shape[0] // n, n <= LANES, row_step)
    for copy in copies[2:]:
        copy.wait()
    known_logits(0, mask, chain, chain_offset, known_start)
    known_logits(1, mask, chain, chain_offset, known_end)


def start_kernel(
    received, pair, queries, keys, values, gates, known, ln_gain, ln_shift, w_bias, w_out, out_bias,
    out, wide, total, narrow, column, packed, apart,
):
    parts, n = out.shape[0], total.shape[1]
    rows = pair.shape[0] // n
    square = rows * rows
    add_bias(False, received, 0, wide, known, total)

    def row_step(row):
        here, broad = block(row, n), block(row, HEADS * n)
        update = attend(
            queries.at[broad, :], keys.at[here, :], values.at[broad, :], gates.at[here, :], total,
            w_out[0], out_bias[0:1, :],
        )
        started = (pair[here, :].astype(F32) + update).astype(BF16).astype(F32)
        column[here, :] = started
        first = row * n
        for place in range(rows):
            packed[pl.ds(row * rows + place, parts, stride=square), :] = column[
                pl.ds(first + place, parts, stride=rows), :
            ]
        normed = layer_norm(started, ln_gain[1:2, :], ln_shift[1:2, :])
        apart[row, :, :] = bias_rows(normed, w_bias, 1)

    each(rows, n <= LANES, row_step)
    for row in range(rows):
        narrow[block(row, HEADS), :] = apart[row, :, :]
    out[:, :square, :] = packed[...].reshape(parts, square, LANES).astype(BF16)
    pack_bias(narrow, square, out)


def end_kernel(
    received, known, ln_gain, ln_shift, w_qkvg, gate_bias, w_out, out_bias, out, wide, total, packed,
    queries, keys, values, gates,
):
    parts, n = received.shape[0], total.shape[1]
    rows = packed.shape[0] // n
    square = rows * rows
    packed[...] = received[:, :square, :].astype(F32).reshape(parts * square, LANES)

    def project_step(place):
        here, broad = block(place, n), block(place, HEADS * n)
        entries = packed[pl.ds(place, n, stride=rows), :]
        normed = layer_norm(entries, ln_gain[1:2, :], ln_shift[1:2, :])
        project(
            normed, w_qkvg[1], gate_bias[1:2, :], queries.at[broad, :], keys.at[here, :],
            values.at[broad, :], gates.at[here, :],
        )

    each(rows, n <= LANES, project_step)
    add_bias(True, received, square, wide, known, total)

    def column_step(place):
        here, broad = block(place, n), block(place, HEADS * n)
        update = attend(
            queries.at[broad, :], keys.at[here, :], values.at[broad, :], gates.at[here, :], total,
            w_out[1], out_bias[1:2, :],
        )
        stripe = pl.ds(place, n, stride=rows)
        packed[stripe, :] = packed[stripe, :] + update

    each(rows, n <= LANES, column_step)
    out[...] = packed[...].astype(BF16)


NEAR = pl.BlockSpec(memory_space=pltpu.VMEM)
FAR = pl.BlockSpec(memory_space=pltpu.HBM)


def call(kernel, out_shape, scratch, far, near):
    far = [pltpu.with_memory_space_constraint(array, pltpu.HBM) for array in far]
    return pl.pallas_call(
        kernel,
        out_shape=out_shape,
        in_specs=[FAR] * len(far) + [NEAR] * len(near),
        out_specs=jax.tree.map(lambda _: NEAR, out_shape),
        scratch_shapes=scratch,
        compiler_params=pltpu.CompilerParams(vmem_limit_bytes=40 * 1024 * 1024),
    )(*far, *near)


def local(
    pair, mask, chain, ln_gain, ln_shift, w_qkvg, gate_bias, w_bias, w_out, out_bias, chain_offset
):
    rows, n = pair.shape[0], pair.shape[1]
    parts = lax.axis_size("row") * lax.axis_size("sub")
    tiles, slots, square = n // LANES, rows * HEADS, rows * rows
    exchange = functools.partial(
        lax.all_to_all, axis_name=("row", "sub"), split_axis=0, concat_axis=0, tiled=True
    )
    shape = jax.ShapeDtypeStruct

    def like(*arrays):
        return [shape(array.shape, array.dtype) for array in arrays]

    flat = pair.reshape(rows * n, C)
    mask_row, chain_row = mask.reshape(1, n), chain.reshape(1, n)
    wide = pltpu.VMEM((parts * slots, LANES), F32)
    total = pltpu.VMEM((HEADS * n, n), F32)
    narrow = pltpu.VMEM((slots, n), F32)
    entries = pltpu.VMEM((rows * n, C), F32)
    bias_part, normed, *early = call(
        bias_kernel,
        [shape((parts, tiles * slots, LANES), BF16), shape((rows * n, C), BF16)]
        + like(flat, ln_gain, ln_shift, w_bias),
        [narrow, pltpu.SemaphoreType.DMA((4,))],
        (flat, ln_gain, ln_shift, w_bias),
        (),
    )
    pair_near, gain_near, shift_near, bias_near = early
    bias_all = exchange(bias_part)
    parted = [
        ((rows * HEADS * n, HD), BF16),
        ((rows * n, HD), BF16),
        ((rows * HEADS * n, 2 * HD), BF16),
        ((rows * n, HD), F32),
    ]
    late = call(
        project_kernel,
        [shape(*each_one) for each_one in parted]
        + [shape((HEADS * n, n), F32)] * 2
        + like(w_qkvg, gate_bias, w_out, out_bias),
        [
            pltpu.SMEM(chain_offset.shape, F32),
            pltpu.VMEM((1, n), jnp.int32),
            pltpu.VMEM((1, n), jnp.int32),
            pltpu.SemaphoreType.DMA((7,)),
        ],
        (chain_offset, mask_row, chain_row, w_qkvg, gate_bias, w_out, out_bias),
        (normed,),
    )
    *projected, known_start, known_end, w_near, gate_near, w_out_near, out_near = late
    sent = call(
        start_kernel,
        shape((parts, square + tiles * slots, LANES), BF16),
        [wide, total, narrow, entries, entries, pltpu.VMEM((rows, HEADS, n), F32)],
        (),
        (
            bias_all, pair_near, *projected, known_start, gain_near, shift_near, bias_near,
            w_out_near, out_near,
        ),
    )
    columns = exchange(sent)
    ended = call(
        end_kernel,
        shape((n * rows, C), BF16),
        [wide, total, entries] + [pltpu.VMEM(*each_one) for each_one in parted],
        (),
        (
            columns, known_end, gain_near, shift_near, w_near, gate_near, w_out_near, out_near
        ),
    )
    return ended.reshape(n, rows, C)


def solution(mesh):
    in_specs = (
        P(("grp", "row", "sub"), None, None),
        P("grp"),
        P("grp"),
        P(),
        P(),
        P(),
        P(),
        P(),
        P(),
        P(),
        P(),
    )
    out_specs = P("grp", ("row", "sub"), None)
    return jax.shard_map(local, mesh=mesh, in_specs=in_specs, out_specs=out_specs, check_vma=False)
```

time: 41.1 us -> 35 us (0.85)
  blocking collectives: 27.4 us -> 11.9 us
  starting transfers between devices: 0 us -> 7.3 us
  waiting for transfers between devices: 0 us -> 6.87 us
  local copies, waits for them, and re-layouts: 3.62 us -> 0 us
  Pallas kernels: 9.72 us -> 8.67 us
    all_to_all x1 -> x0, blocking collectives: 15.5 us -> none  [local(): bias_all = exchange(bias_part)]
    all_to_all x0 -> x1, starting transfers between devices: none -> 7.3 us  [local(): bias_all = exchange(bias_part)]
    all_to_all x0 -> x1, waiting for transfers between devices: none -> 6.87 us  [local(): bias_all = exchange(bias_part)]
    unnamed x24 -> x0, local copies, waits for them, and re-layouts: 3.62 us -> none
    pallas_call x3 -> x4, Pallas kernels: 9.72 us -> 8.67 us  [call(): pl.pallas_call(kernel, out_shape=out_shape, in_specs=[FAR] * len(far) + [...]
  transfers between devices with their start and end apart: 0 -> 1, of which waited for: 0 -> 1; matrix products, arithmetic and copies ran while one was open for 0% -> 0% of each run, Pallas kernels for 0% -> 4%
where the time goes in v2:
time: 35 us; the launch traced here: 34.8 us
  blocking collectives  11.9 us (34%)
  Pallas kernels  8.67 us (25%)
  starting transfers between devices  7.3 us (21%)
  waiting for transfers between devices  6.87 us (20%)
    all_to_all x1, blocking collectives, local(): columns = exchange(sent)  11.9 us
    pallas_call x4, Pallas kernels, call(): pl.pallas_call(kernel, out_shape=out_shape, in_specs=[FAR] * len(far) + [...  8.67 us
    all_to_all x1, starting transfers between devices, local(): bias_all = exchange(bias_part)  7.3 us
    all_to_all x1, waiting for transfers between devices, local(): bias_all = exchange(bias_part)  6.87 us
  transfers between devices with their start and end apart: 1, of which 1 were waited for; matrix products, arithmetic and copies ran while one was open for 0% of the time, Pallas kernels for 4%

profile of v2, /device:TPU:0, one launch (start us, length us, event | category | flops | bytes accessed | tf_op | source)
XLA Modules:
  0.0 34.8 jit_solution(4450289421459293269)
XLA Ops:
  0.0 2.0 %shard_map.109 = (bf16[32,16,128]{2,1,0:T(8,128)(2,1)}, bf16[512,128]{1,0:T(8,128)(2,1)S(1)}, bf16[512,128]{1,0:T(8,128)(2,1)S(1)}, f32[2,128]{1,0:T(2,128)S(1)}...) custom-call(bf16[512,128]{1,0:T(8,128)(2,1)} %bitcast.4, f32[2,128]{1,0:T(2,128)} %gain_far.1, f32[2,128]{1,0:T(2,128)} %shift_far.1, ...), custom_call_target="tpu_custom_call" | custom-call | tf_op jit(solution)/shard_map/pallas_call | solution.py:244
  2.0 7.3 %all-to-all-start = ((bf16[32,16,128]{2,1,0:T(8,128)(2,1)}), bf16[32,16,128]{2,1,0:T(8,128)(2,1)S(1)}, u32[]{:S(2)}, u32[]{:S(2)}) async-start(bf16[32,16,128]{2,1,0:T(8,128)(2,1)} %get-tuple-element.21), calls=%async_computation | async-start | bytes 262144 | tf_op jit(solution)/shard_map/all_to_all | solution.py:283
  9.3 1.5 %shard_map.110 = (bf16[2048,128]{1,0:T(8,128)(2,1)S(1)}, bf16[512,128]{1,0:T(8,128)(2,1)S(1)}, bf16[2048,256]{1,0:T(8,128)(2,1)S(1)}, f32[512,128]{1,0:T(8,128)S...) custom-call(f32[2,4]{1,0:T(2,128)} %offset_far.1, ...), custom_call_target="tpu_custom_call" | custom-call | tf_op jit(solution)/shard_map/pallas_call | solution.py:244
  10.9 6.9 %all-to-all-done.received = bf16[32,16,128]{2,1,0:T(8,128)(2,1)S(1)} async-done(((bf16[32,16,128]{2,1,0:T(8,128)(2,1)}), bf16[32,16,128]{2,1,0:T(8,128)(2,1)S(1)}, u32[]{:S(2)}, u32[]{:S(2)}) %all-to-all-start) | async-done | bytes 131104 | tf_op jit(solution)/shard_map/all_to_all | solution.py:283
  17.7 2.4 %shard_map.111 = bf16[32,32,128]{2,1,0:T(8,128)(2,1)S(1)} custom-call(bf16[32,16,128]{2,1,0:T(8,128)(2,1)S(1)} %all-to-all-done.received, bf16[512,128]{1,0:T(8,128)(2,1)S(1)} %get-tuple-element.22.pair, bf16[2048,128]{1,0:T(8,128)(2,1)S(1)} %get-tuple-element.24.queries, bf16[512,128]{1,0:T(8,128)(2,1)S(1)} %get-tuple-element.25.keys, ...), custom_call_target="tpu_custom_call" | custom-call | tf_op jit(solution)/shard_map/pallas_call | solution.py:244
  20.2 11.9 %all_to_all.10.received = bf16[32,32,128]{2,1,0:T(8,128)(2,1)S(1)} all-to-all(bf16[32,32,128]{2,1,0:T(8,128)(2,1)S(1)} %shard_map.111), channel_id=1, replica_groups=mesh['grp'=1,'row'=8,'sub'=4] {'row','sub'}, dimensions={0} | all-to-all | bytes 524288 | tf_op jit(solution)/shard_map/all_to_all | solution.py:315
  32.1 2.7 %shard_map.112 = bf16[512,128]{1,0:T(8,128)(2,1)} custom-call(bf16[32,32,128]{2,1,0:T(8,128)(2,1)S(1)} %all_to_all.10.received, f32[512,128]{1,0:T(8,128)S(1)} %get-tuple-element.34.known, f32[2,128]{1,0:T(2,128)S(1)} %get-tuple-element.29.ln_gain, f32[2,128]{1,0:T(2,128)S(1)} %get-tuple-element.30.ln_shift, ...), custom_call_target="tpu_custom_call" | custom-call | tf_op jit(solution)/shard_map/pallas_call | solution.py:244
Async XLA Ops:
  2.0 15.7 %all-to-all-start = ((bf16[32,16,128]{2,1,0:T(8,128)(2,1)}), bf16[32,16,128]{2,1,0:T(8,128)(2,1)S(1)}, u32[]{:S(2)}, u32[]{:S(2)}) async-start(bf16[32,16,128]{2,1,0:T(8,128)(2,1)} %get-tuple-element.21), calls=%async_computation | async-start | bytes 262144 | tf_op jit(solution)/shard_map/all_to_all | solution.py:283

commit v3 on v2

--- a/solution.py
+++ b/solution.py
@@ -97,18 +97,36 @@
         values[block(head, n), HD:] = jnp.broadcast_to(own.astype(BF16), (n, HD))
 
 
-def attend(queries, keys, values, gates, total, w_out, out_row):
+def attend(queries, keys, values, gates, total):
     n = keys.shape[0]
     logits = matmul(queries[...], keys[...], NT) + total[...]
     expon = jnp.exp(logits - jnp.max(logits, axis=-1, keepdims=True)).astype(BF16)
     beside = jnp.concatenate([expon[block(head, n), :] for head in range(HEADS)], axis=1)
     summed = matmul(beside, values[...])
-    gated = (summed[:, :HD] / summed[:, HD:] * gates[...]).astype(BF16)
-    return matmul(gated, w_out) + out_row
-
-
-def bias_rows(normed, w_bias, layer):
-    return matmul(w_bias[layer], normed, NT)
+    return (summed[:, :HD] / summed[:, HD:] * gates[...]).astype(BF16)
+
+
+def attend_all(queries, keys, values, gates, total, gated):
+    n = total.shape[1]
+
+    def step(index):
+        here, broad = block(index, n), block(index, HEADS * n)
+        gated[here, :] = attend(
+            queries.at[broad, :], keys.at[here, :], values.at[broad, :], gates.at[here, :], total
+        )
+
+    each(keys.shape[0] // n, n <= LANES, step)
+
+
+def bias_rows(entries, layer, ln_gain, ln_shift, w_bias, narrow):
+    normed = layer_norm(
+        entries, ln_gain[layer : layer + 1, :], ln_shift[layer : layer + 1, :]
+    )
+    bias = matmul(w_bias[layer], normed, NT)
+    n = narrow.shape[1]
+    for row in range(entries.shape[0] // n):
+        narrow[block(row, HEADS), :] = bias[:, block(row, n)]
+    return normed
 
 
 def pack_bias(narrow, first_slot, out):
@@ -131,15 +149,10 @@
 def bias_kernel(
     pair_far, gain_far, shift_far, bias_far, out, normed_out, pair, ln_gain, ln_shift, w_bias, narrow, sems
 ):
-    n = narrow.shape[1]
     far, near = (pair_far, gain_far, shift_far, bias_far), (pair, ln_gain, ln_shift, w_bias)
     for copy in fetch(zip(far, near, strict=True), sems):
         copy.wait()
-    for row in range(pair.shape[0] // n):
-        entries = pair[block(row, n), :].astype(F32)
-        normed = layer_norm(entries, ln_gain[0:1, :], ln_shift[0:1, :])
-        normed_out[block(row, n), :] = normed
-        narrow[block(row, HEADS), :] = bias_rows(normed, w_bias, 0)
+    normed_out[...] = bias_rows(pair[...].astype(F32), 0, ln_gain, ln_shift, w_bias, narrow)
     pack_bias(narrow, 0, out)
 
 
@@ -171,39 +184,29 @@
 
 def start_kernel(
     received, pair, queries, keys, values, gates, known, ln_gain, ln_shift, w_bias, w_out, out_bias,
-    out, wide, total, narrow, column, packed, apart,
+    out, wide, total, gated, narrow, column, packed,
 ):
     parts, n = out.shape[0], total.shape[1]
     rows = pair.shape[0] // n
     square = rows * rows
     add_bias(False, received, 0, wide, known, total)
-
-    def row_step(row):
-        here, broad = block(row, n), block(row, HEADS * n)
-        update = attend(
-            queries.at[broad, :], keys.at[here, :], values.at[broad, :], gates.at[here, :], total,
-            w_out[0], out_bias[0:1, :],
-        )
-        started = (pair[here, :].astype(F32) + update).astype(BF16).astype(F32)
-        column[here, :] = started
-        first = row * n
+    attend_all(queries, keys, values, gates, total, gated)
+    update = matmul(gated[...], w_out[0]) + out_bias[0:1, :]
+    started = (pair[...].astype(F32) + update).astype(BF16).astype(F32)
+    column[...] = started
+    bias_rows(started, 1, ln_gain, ln_shift, w_bias, narrow)
+    for row in range(rows):
         for place in range(rows):
             packed[pl.ds(row * rows + place, parts, stride=square), :] = column[
-                pl.ds(first + place, parts, stride=rows), :
+                pl.ds(row * n + place, parts, stride=rows), :
             ]
-        normed = layer_norm(started, ln_gain[1:2, :], ln_shift[1:2, :])
-        apart[row, :, :] = bias_rows(normed, w_bias, 1)
-
-    each(rows, n <= LANES, row_step)
-    for row in range(rows):
-        narrow[block(row, HEADS), :] = apart[row, :, :]
     out[:, :square, :] = packed[...].reshape(parts, square, LANES).astype(BF16)
     pack_bias(narrow, square, out)
 
 
 def end_kernel(
-    received, known, ln_gain, ln_shift, w_qkvg, gate_bias, w_out, out_bias, out, wide, total, packed,
-    queries, keys, values, gates,
+    received, known, ln_gain, ln_shift, w_qkvg, gate_bias, w_out, out_bias, out, wide, total, gated,
+    packed, queries, keys, values, gates,
 ):
     parts, n = received.shape[0], total.shape[1]
     rows = packed.shape[0] // n
@@ -221,17 +224,11 @@
 
     each(rows, n <= LANES, project_step)
     add_bias(True, received, square, wide, known, total)
-
-    def column_step(place):
-        here, broad = block(place, n), block(place, HEADS * n)
-        update = attend(
-            queries.at[broad, :], keys.at[here, :], values.at[broad, :], gates.at[here, :], total,
-            w_out[1], out_bias[1:2, :],
-        )
+    attend_all(queries, keys, values, gates, total, gated)
+    update = matmul(gated[...], w_out[1]) + out_bias[1:2, :]
+    for place in range(rows):
         stripe = pl.ds(place, n, stride=rows)
-        packed[stripe, :] = packed[stripe, :] + update
-
-    each(rows, n <= LANES, column_step)
+        packed[stripe, :] = packed[stripe, :] + update[block(place, n), :]
     out[...] = packed[...].astype(BF16)
 
 
@@ -270,6 +267,7 @@
     wide = pltpu.VMEM((parts * slots, LANES), F32)
     total = pltpu.VMEM((HEADS * n, n), F32)
     narrow = pltpu.VMEM((slots, n), F32)
+    gated = pltpu.VMEM((rows * n, HD), BF16)
     entries = pltpu.VMEM((rows * n, C), F32)
     bias_part, normed, *early = call(
         bias_kernel,
@@ -305,7 +303,7 @@
     sent = call(
         start_kernel,
         shape((parts, square + tiles * slots, LANES), BF16),
-        [wide, total, narrow, entries, entries, pltpu.VMEM((rows, HEADS, n), F32)],
+        [wide, total, gated, narrow, entries, entries],
         (),
         (
             bias_all, pair_near, *projected, known_start, gain_near, shift_near, bias_near,
@@ -316,7 +314,7 @@
     ended = call(
         end_kernel,
         shape((n * rows, C), BF16),
-        [wide, total, entries] + [pltpu.VMEM(*each_one) for each_one in parted],
+        [wide, total, gated, entries] + [pltpu.VMEM(*each_one) for each_one in parted],
         (),
         (
             columns, known_end, gain_near, shift_near, w_near, gate_near, w_out_near, out_near

time: 35 us -> 33 us (0.943)
  Pallas kernels: 8.67 us -> 6.66 us
    pallas_call x4, Pallas kernels: 8.67 us -> 6.66 us  [call(): pl.pallas_call(kernel, out_shape=out_shape, in_specs=[FAR] * len(far) + [...]
  transfers between devices with their start and end apart: 1 -> 1, of which waited for: 1 -> 1; matrix products, arithmetic and copies ran while one was open for 0% -> 0% of each run, Pallas kernels for 4% -> 5%
where the time goes in v3:
time: 33 us; the launch traced here: 32.8 us
  blocking collectives  11.9 us (36%)
  starting transfers between devices  7.3 us (22%)
  waiting for transfers between devices  6.88 us (21%)
  Pallas kernels  6.66 us (20%)
    all_to_all x1, blocking collectives, local(): columns = exchange(sent)  11.9 us
    all_to_all x1, starting transfers between devices, local(): bias_all = exchange(bias_part)  7.3 us
    all_to_all x1, waiting for transfers between devices, local(): bias_all = exchange(bias_part)  6.88 us
    pallas_call x4, Pallas kernels, call(): pl.pallas_call(kernel, out_shape=out_shape, in_specs=[FAR] * len(far) + [...  6.66 us
  transfers between devices with their start and end apart: 1, of which 1 were waited for; matrix products, arithmetic and copies ran while one was open for 0% of the time, Pallas kernels for 5%

profile of v3, /device:TPU:0, one launch (start us, length us, event | category | flops | bytes accessed | tf_op | source)
XLA Modules:
  0.0 32.8 jit_solution(6233360622624225044)
XLA Ops:
  0.0 2.0 %shard_map.109 = (bf16[32,16,128]{2,1,0:T(8,128)(2,1)}, bf16[512,128]{1,0:T(8,128)(2,1)S(1)}, bf16[512,128]{1,0:T(8,128)(2,1)S(1)}, f32[2,128]{1,0:T(2,128)S(1)}...) custom-call(bf16[512,128]{1,0:T(8,128)(2,1)} %bitcast.4, f32[2,128]{1,0:T(2,128)} %gain_far.1, f32[2,128]{1,0:T(2,128)} %shift_far.1, ...), custom_call_target="tpu_custom_call" | custom-call | tf_op jit(solution)/shard_map/pallas_call | solution.py:241
  2.0 7.3 %all-to-all-start = ((bf16[32,16,128]{2,1,0:T(8,128)(2,1)}), bf16[32,16,128]{2,1,0:T(8,128)(2,1)S(1)}, u32[]{:S(2)}, u32[]{:S(2)}) async-start(bf16[32,16,128]{2,1,0:T(8,128)(2,1)} %get-tuple-element.21), calls=%async_computation | async-start | bytes 262144 | tf_op jit(solution)/shard_map/all_to_all | solution.py:281
  9.3 1.5 %shard_map.110 = (bf16[2048,128]{1,0:T(8,128)(2,1)S(1)}, bf16[512,128]{1,0:T(8,128)(2,1)S(1)}, bf16[2048,256]{1,0:T(8,128)(2,1)S(1)}, f32[512,128]{1,0:T(8,128)S...) custom-call(f32[2,4]{1,0:T(2,128)} %offset_far.1, ...), custom_call_target="tpu_custom_call" | custom-call | tf_op jit(solution)/shard_map/pallas_call | solution.py:241
  10.8 6.9 %all-to-all-done.received = bf16[32,16,128]{2,1,0:T(8,128)(2,1)S(1)} async-done(((bf16[32,16,128]{2,1,0:T(8,128)(2,1)}), bf16[32,16,128]{2,1,0:T(8,128)(2,1)S(1)}, u32[]{:S(2)}, u32[]{:S(2)}) %all-to-all-start) | async-done | bytes 131104 | tf_op jit(solution)/shard_map/all_to_all | solution.py:281
  17.7 1.1 %shard_map.111 = bf16[32,32,128]{2,1,0:T(8,128)(2,1)S(1)} custom-call(bf16[32,16,128]{2,1,0:T(8,128)(2,1)S(1)} %all-to-all-done.received, bf16[512,128]{1,0:T(8,128)(2,1)S(1)} %get-tuple-element.22.pair, bf16[2048,128]{1,0:T(8,128)(2,1)S(1)} %get-tuple-element.24.queries, bf16[512,128]{1,0:T(8,128)(2,1)S(1)} %get-tuple-element.25.keys, ...), custom_call_target="tpu_custom_call" | custom-call | tf_op jit(solution)/shard_map/pallas_call | solution.py:241
  18.8 11.9 %all_to_all.10.received = bf16[32,32,128]{2,1,0:T(8,128)(2,1)S(1)} all-to-all(bf16[32,32,128]{2,1,0:T(8,128)(2,1)S(1)} %shard_map.111), channel_id=1, replica_groups=mesh['grp'=1,'row'=8,'sub'=4] {'row','sub'}, dimensions={0} | all-to-all | bytes 524288 | tf_op jit(solution)/shard_map/all_to_all | solution.py:313
  30.7 2.1 %shard_map.112 = bf16[512,128]{1,0:T(8,128)(2,1)} custom-call(bf16[32,32,128]{2,1,0:T(8,128)(2,1)S(1)} %all_to_all.10.received, f32[512,128]{1,0:T(8,128)S(1)} %get-tuple-element.34.known, f32[2,128]{1,0:T(2,128)S(1)} %get-tuple-element.29.ln_gain, f32[2,128]{1,0:T(2,128)S(1)} %get-tuple-element.30.ln_shift, ...), custom_call_target="tpu_custom_call" | custom-call | tf_op jit(solution)/shard_map/pallas_call | solution.py:241
Async XLA Ops:
  2.0 15.7 %all-to-all-start = ((bf16[32,16,128]{2,1,0:T(8,128)(2,1)}), bf16[32,16,128]{2,1,0:T(8,128)(2,1)S(1)}, u32[]{:S(2)}, u32[]{:S(2)}) async-start(bf16[32,16,128]{2,1,0:T(8,128)(2,1)} %get-tuple-element.21), calls=%async_computation | async-start | bytes 262144 | tf_op jit(solution)/shard_map/all_to_all | solution.py:281

commit v4 on v3

--- a/solution.py
+++ b/solution.py
@@ -66,21 +66,21 @@
         total[block(head, n), :] = jnp.where(cross, chain_offset[layer, head], 0.0) + key_row
 
 
-def add_bias(flip, received, first_slot, wide, known, total):
+def add_bias(order, received, first_slot, wide, total, known=None):
     n = total.shape[1]
-    parts, slots = received.shape[0], wide.shape[0] // received.shape[0]
+    slots = wide.shape[0] // received.shape[0]
     for tile in range(n // LANES):
         first = first_slot + tile * slots
-        wide[...] = received[:, first : first + slots, :].astype(F32).reshape(parts * slots, LANES)
+        for place, part in enumerate(order):
+            wide[block(part, slots), :] = received[place, first : first + slots, :].astype(F32)
         span = block(tile, LANES)
         for head in range(HEADS):
             gathered = wide[pl.ds(head, n, stride=HEADS), :]
-            if flip:
+            if known is not None:
                 here = block(head * (n // LANES) + tile, LANES)
                 total[here, :] = gathered.T + known[here, :]
             else:
-                here = block(head, n)
-                total[here, span] = gathered + known[here, span]
+                total[block(head, n), span] = gathered
 
 
 def project(normed, weights, gate_row, queries, keys, values, gates):
@@ -97,25 +97,12 @@
         values[block(head, n), HD:] = jnp.broadcast_to(own.astype(BF16), (n, HD))
 
 
-def attend(queries, keys, values, gates, total):
-    n = keys.shape[0]
-    logits = matmul(queries[...], keys[...], NT) + total[...]
+def attend(logits, values, gates):
+    n = logits.shape[1]
     expon = jnp.exp(logits - jnp.max(logits, axis=-1, keepdims=True)).astype(BF16)
     beside = jnp.concatenate([expon[block(head, n), :] for head in range(HEADS)], axis=1)
-    summed = matmul(beside, values[...])
-    return (summed[:, :HD] / summed[:, HD:] * gates[...]).astype(BF16)
-
-
-def attend_all(queries, keys, values, gates, total, gated):
-    n = total.shape[1]
-
-    def step(index):
-        here, broad = block(index, n), block(index, HEADS * n)
-        gated[here, :] = attend(
-            queries.at[broad, :], keys.at[here, :], values.at[broad, :], gates.at[here, :], total
-        )
-
-    each(keys.shape[0] // n, n <= LANES, step)
+    summed = matmul(beside, values)
+    return (summed[:, :HD] / summed[:, HD:] * gates).astype(BF16)
 
 
 def bias_rows(entries, layer, ln_gain, ln_shift, w_bias, narrow):
@@ -158,15 +145,17 @@
 
 def project_kernel(
     offset_far, mask_far, chain_far, w_far, gate_far, w_out_far, out_bias_far, normed,
-    queries, keys, values, gates, known_start, known_end, w_qkvg, gate_bias, w_out, out_bias,
-    chain_offset, mask, chain, sems,
+    logits, values, gates, known_end, w_qkvg, gate_bias, w_out, out_bias,
+    chain_offset, mask, chain, known_start, queries, keys, sems,
 ):
     n = known_start.shape[1]
     far = (w_far, gate_far, offset_far, mask_far, chain_far, w_out_far, out_bias_far)
     near = (w_qkvg, gate_bias, chain_offset, mask, chain, w_out, out_bias)
     copies = fetch(zip(far, near, strict=True), sems)
-    copies[0].wait()
-    copies[1].wait()
+    for copy in copies:
+        copy.wait()
+    known_logits(0, mask, chain, chain_offset, known_start)
+    known_logits(1, mask, chain, chain_offset, known_end)
 
     def row_step(row):
         here, wide = block(row, n), block(row, HEADS * n)
@@ -174,23 +163,25 @@
             normed[here, :], w_qkvg[0], gate_bias[0:1, :], queries.at[wide, :], keys.at[here, :],
             values.at[wide, :], gates.at[here, :],
         )
+        logits[wide, :] = matmul(queries[wide, :], keys[here, :], NT) + known_start[...]
 
     each(keys.shape[0] // n, n <= LANES, row_step)
-    for copy in copies[2:]:
-        copy.wait()
-    known_logits(0, mask, chain, chain_offset, known_start)
-    known_logits(1, mask, chain, chain_offset, known_end)
 
 
 def start_kernel(
-    received, pair, queries, keys, values, gates, known, ln_gain, ln_shift, w_bias, w_out, out_bias,
-    out, wide, total, gated, narrow, column, packed,
+    first_order, second_order, received, pair, logits, values, gates, ln_gain, ln_shift, w_bias, w_out,
+    out_bias, out, wide, total, gated, narrow, column, packed,
 ):
     parts, n = out.shape[0], total.shape[1]
     rows = pair.shape[0] // n
     square = rows * rows
-    add_bias(False, received, 0, wide, known, total)
-    attend_all(queries, keys, values, gates, total, gated)
+    add_bias(first_order, received, 0, wide, total)
+
+    def row_step(row):
+        here, broad = block(row, n), block(row, HEADS * n)
+        gated[here, :] = attend(logits[broad, :] + total[...], values[broad, :], gates[here, :])
+
+    each(rows, n <= LANES, row_step)
     update = matmul(gated[...], w_out[0]) + out_bias[0:1, :]
     started = (pair[...].astype(F32) + update).astype(BF16).astype(F32)
     column[...] = started
@@ -200,18 +191,20 @@
             packed[pl.ds(row * rows + place, parts, stride=square), :] = column[
                 pl.ds(row * n + place, parts, stride=rows), :
             ]
-    out[:, :square, :] = packed[...].reshape(parts, square, LANES).astype(BF16)
+    for place, part in enumerate(second_order):
+        out[place, :square, :] = packed[block(part, square), :].astype(BF16)
     pack_bias(narrow, square, out)
 
 
 def end_kernel(
-    received, known, ln_gain, ln_shift, w_qkvg, gate_bias, w_out, out_bias, out, wide, total, gated,
+    order, received, known, ln_gain, ln_shift, w_qkvg, gate_bias, w_out, out_bias, out, wide, total, gated,
     packed, queries, keys, values, gates,
 ):
     parts, n = received.shape[0], total.shape[1]
     rows = packed.shape[0] // n
     square = rows * rows
-    packed[...] = received[:, :square, :].astype(F32).reshape(parts * square, LANES)
+    for place, part in enumerate(order):
+        packed[block(part, square), :] = received[place, :square, :].astype(F32)
 
     def project_step(place):
         here, broad = block(place, n), block(place, HEADS * n)
@@ -223,8 +216,14 @@
         )
 
     each(rows, n <= LANES, project_step)
-    add_bias(True, received, square, wide, known, total)
-    attend_all(queries, keys, values, gates, total, gated)
+    add_bias(order, received, square, wide, total, known)
+
+    def column_step(place):
+        here, broad = block(place, n), block(place, HEADS * n)
+        logits = matmul(queries[broad, :], keys[here, :], NT) + total[...]
+        gated[here, :] = attend(logits, values[broad, :], gates[here, :])
+
+    each(rows, n <= LANES, column_step)
     update = matmul(gated[...], w_out[1]) + out_bias[1:2, :]
     for place in range(rows):
         stripe = pl.ds(place, n, stride=rows)
@@ -248,15 +247,24 @@
     )(*far, *near)
 
 
+def exchange(array, order):
+    return lax.all_to_all(
+        array, ("row", "sub"), split_axis=0, concat_axis=0, tiled=True, axis_index_groups=[order]
+    )
+
+
+def orders(outer, inner):
+    natural = list(range(outer * inner))
+    return natural[::-1], natural
+
+
 def local(
     pair, mask, chain, ln_gain, ln_shift, w_qkvg, gate_bias, w_bias, w_out, out_bias, chain_offset
 ):
     rows, n = pair.shape[0], pair.shape[1]
     parts = lax.axis_size("row") * lax.axis_size("sub")
     tiles, slots, square = n // LANES, rows * HEADS, rows * rows
-    exchange = functools.partial(
-        lax.all_to_all, axis_name=("row", "sub"), split_axis=0, concat_axis=0, tiled=True
-    )
+    first_order, second_order = orders(lax.axis_size("row"), lax.axis_size("sub"))
     shape = jax.ShapeDtypeStruct
 
     def like(*arrays):
@@ -278,43 +286,40 @@
         (),
     )
     pair_near, gain_near, shift_near, bias_near = early
-    bias_all = exchange(bias_part)
-    parted = [
-        ((rows * HEADS * n, HD), BF16),
-        ((rows * n, HD), BF16),
-        ((rows * HEADS * n, 2 * HD), BF16),
-        ((rows * n, HD), F32),
-    ]
+    bias_all = exchange(bias_part, first_order)
+    queries, keys = ((rows * HEADS * n, HD), BF16), ((rows * n, HD), BF16)
+    values, gates = ((rows * HEADS * n, 2 * HD), BF16), ((rows * n, HD), F32)
     late = call(
         project_kernel,
-        [shape(*each_one) for each_one in parted]
-        + [shape((HEADS * n, n), F32)] * 2
+        [shape((rows * HEADS * n, n), F32), shape(*values), shape(*gates), shape((HEADS * n, n), F32)]
         + like(w_qkvg, gate_bias, w_out, out_bias),
         [
             pltpu.SMEM(chain_offset.shape, F32),
             pltpu.VMEM((1, n), jnp.int32),
             pltpu.VMEM((1, n), jnp.int32),
+            total,
+            pltpu.VMEM(*queries),
+            pltpu.VMEM(*keys),
             pltpu.SemaphoreType.DMA((7,)),
         ],
         (chain_offset, mask_row, chain_row, w_qkvg, gate_bias, w_out, out_bias),
         (normed,),
     )
-    *projected, known_start, known_end, w_near, gate_near, w_out_near, out_near = late
+    *projected, known_end, w_near, gate_near, w_out_near, out_near = late
     sent = call(
-        start_kernel,
+        functools.partial(start_kernel, first_order, second_order),
         shape((parts, square + tiles * slots, LANES), BF16),
         [wide, total, gated, narrow, entries, entries],
         (),
         (
-            bias_all, pair_near, *projected, known_start, gain_near, shift_near, bias_near,
-            w_out_near, out_near,
+            bias_all, pair_near, *projected, gain_near, shift_near, bias_near, w_out_near, out_near
         ),
     )
-    columns = exchange(sent)
+    columns = exchange(sent, second_order)
     ended = call(
-        end_kernel,
+        functools.partial(end_kernel, second_order),
         shape((n * rows, C), BF16),
-        [wide, total, gated, entries] + [pltpu.VMEM(*each_one) for each_one in parted],
+        [wide, total, gated, entries] + [pltpu.VMEM(*each_one) for each_one in (queries, keys, values, gates)],
         (),
         (
             columns, known_end, gain_near, shift_near, w_near, gate_near, w_out_near, out_near

time: 33 us -> 32.5 us (0.985)
  waiting for transfers between devices: 6.88 us -> 6.04 us
    all_to_all x1, waiting for transfers between devices: 6.88 us -> 6.04 us  [exchange(): lax.all_to_all(array, ('row', 'sub'), split_axis=0, concat_axis=0, tiled=...]
  transfers between devices with their start and end apart: 1 -> 1, of which waited for: 1 -> 1; matrix products, arithmetic and copies ran while one was open for 0% -> 0% of each run, Pallas kernels for 5% -> 6%
where the time goes in v4:
time: 32.5 us; the launch traced here: 32.3 us
  blocking collectives  12.1 us (37%)
  starting transfers between devices  7.3 us (22%)
  Pallas kernels  6.82 us (21%)
  waiting for transfers between devices  6.04 us (19%)
    all_to_all x1, blocking collectives, exchange(): lax.all_to_all(array, ('row', 'sub'), split_axis=0, concat_axis=0, tiled=...  12.1 us
    all_to_all x1, starting transfers between devices, exchange(): lax.all_to_all(array, ('row', 'sub'), split_axis=0, concat_axis=0, tiled=...  7.3 us
    pallas_call x4, Pallas kernels, call(): pl.pallas_call(kernel, out_shape=out_shape, in_specs=[FAR] * len(far) + [...  6.82 us
    all_to_all x1, waiting for transfers between devices, exchange(): lax.all_to_all(array, ('row', 'sub'), split_axis=0, concat_axis=0, tiled=...  6.04 us
  transfers between devices with their start and end apart: 1, of which 1 were waited for; matrix products, arithmetic and copies ran while one was open for 0% of the time, Pallas kernels for 6%

profile of v4, /device:TPU:0, one launch (start us, length us, event | category | flops | bytes accessed | tf_op | source)
XLA Modules:
  0.0 32.3 jit_solution(18095162634885130709)
XLA Ops:
  0.0 2.0 %shard_map.109 = (bf16[32,16,128]{2,1,0:T(8,128)(2,1)}, bf16[512,128]{1,0:T(8,128)(2,1)S(1)}, bf16[512,128]{1,0:T(8,128)(2,1)S(1)}, f32[2,128]{1,0:T(2,128)S(1)}...) custom-call(bf16[512,128]{1,0:T(8,128)(2,1)} %bitcast.4, f32[2,128]{1,0:T(2,128)} %gain_far.1, f32[2,128]{1,0:T(2,128)} %shift_far.1, ...), custom_call_target="tpu_custom_call" | custom-call | tf_op jit(solution)/shard_map/pallas_call | solution.py:240
  2.0 7.3 %all-to-all-start = ((bf16[32,16,128]{2,1,0:T(8,128)(2,1)}), bf16[32,16,128]{2,1,0:T(8,128)(2,1)S(1)}, u32[]{:S(2)}, u32[]{:S(2)}) async-start(bf16[32,16,128]{2,1,0:T(8,128)(2,1)} %get-tuple-element.19), calls=%async_computation | async-start | bytes 262144 | tf_op jit(solution)/shard_map/all_to_all | solution.py:251
  9.3 1.8 %shard_map.110 = (f32[2048,128]{1,0:T(8,128)S(1)}, bf16[2048,256]{1,0:T(8,128)(2,1)S(1)}, f32[512,128]{1,0:T(8,128)S(1)}, f32[512,128]{1,0:T(8,128)S(1)}, bf16[2...) custom-call(f32[2,4]{1,0:T(2,128)} %offset_far.1, ...), custom_call_target="tpu_custom_call" | custom-call | tf_op jit(solution)/shard_map/pallas_call | solution.py:240
  11.1 6.0 %all-to-all-done.received = bf16[32,16,128]{2,1,0:T(8,128)(2,1)S(1)} async-done(((bf16[32,16,128]{2,1,0:T(8,128)(2,1)}), bf16[32,16,128]{2,1,0:T(8,128)(2,1)S(1)}, u32[]{:S(2)}, u32[]{:S(2)}) %all-to-all-start) | async-done | bytes 131104 | tf_op jit(solution)/shard_map/all_to_all | solution.py:251
  17.1 1.0 %shard_map.111 = bf16[32,32,128]{2,1,0:T(8,128)(2,1)S(1)} custom-call(bf16[32,16,128]{2,1,0:T(8,128)(2,1)S(1)} %all-to-all-done.received, bf16[512,128]{1,0:T(8,128)(2,1)S(1)} %get-tuple-element.20.pair, f32[2048,128]{1,0:T(8,128)S(1)} %get-tuple-element.22.logits, bf16[2048,256]{1,0:T(8,128)(2,1)S(1)} %get-tuple-element.23.values, ...), custom_call_target="tpu_custom_call" | custom-call | tf_op jit(solution)/shard_map/pallas_call | solution.py:240
  18.1 12.1 %all_to_all.10.received = bf16[32,32,128]{2,1,0:T(8,128)(2,1)S(1)} all-to-all(bf16[32,32,128]{2,1,0:T(8,128)(2,1)S(1)} %shard_map.111), channel_id=1, replica_groups={{0,1,2,3,4,5,6,7,8,9,10,11,12,13,14,15,16,17,18,19,20,21,22,23,24,25,26..., dimensions={0} | all-to-all | bytes 524288 | tf_op jit(solution)/shard_map/all_to_all | solution.py:251
  30.3 2.1 %shard_map.112 = bf16[512,128]{1,0:T(8,128)(2,1)} custom-call(bf16[32,32,128]{2,1,0:T(8,128)(2,1)S(1)} %all_to_all.10.received, f32[512,128]{1,0:T(8,128)S(1)} %get-tuple-element.30.known, f32[2,128]{1,0:T(2,128)S(1)} %get-tuple-element.25.ln_gain, f32[2,128]{1,0:T(2,128)S(1)} %get-tuple-element.26.ln_shift, ...), custom_call_target="tpu_custom_call" | custom-call | tf_op jit(solution)/shard_map/pallas_call | solution.py:240
Async XLA Ops:
  2.0 15.2 %all-to-all-start = ((bf16[32,16,128]{2,1,0:T(8,128)(2,1)}), bf16[32,16,128]{2,1,0:T(8,128)(2,1)S(1)}, u32[]{:S(2)}, u32[]{:S(2)}) async-start(bf16[32,16,128]{2,1,0:T(8,128)(2,1)} %get-tuple-element.19), calls=%async_computation | async-start | bytes 262144 | tf_op jit(solution)/shard_map/all_to_all | solution.py:251

commit v5 on v4

--- a/solution.py
+++ b/solution.py
@@ -66,7 +66,7 @@
         total[block(head, n), :] = jnp.where(cross, chain_offset[layer, head], 0.0) + key_row
 
 
-def add_bias(order, received, first_slot, wide, total, known=None):
+def add_bias(flip, order, received, first_slot, wide, known, total):
     n = total.shape[1]
     slots = wide.shape[0] // received.shape[0]
     for tile in range(n // LANES):
@@ -76,11 +76,12 @@
         span = block(tile, LANES)
         for head in range(HEADS):
             gathered = wide[pl.ds(head, n, stride=HEADS), :]
-            if known is not None:
+            if flip:
                 here = block(head * (n // LANES) + tile, LANES)
                 total[here, :] = gathered.T + known[here, :]
             else:
-                total[block(head, n), span] = gathered
+                here = block(head, n)
+                total[here, span] = gathered + known[here, span]
 
 
 def project(normed, weights, gate_row, queries, keys, values, gates):
@@ -97,12 +98,25 @@
         values[block(head, n), HD:] = jnp.broadcast_to(own.astype(BF16), (n, HD))
 
 
-def attend(logits, values, gates):
-    n = logits.shape[1]
+def attend(queries, keys, values, gates, total):
+    n = keys.shape[0]
+    logits = matmul(queries[...], keys[...], NT) + total[...]
     expon = jnp.exp(logits - jnp.max(logits, axis=-1, keepdims=True)).astype(BF16)
     beside = jnp.concatenate([expon[block(head, n), :] for head in range(HEADS)], axis=1)
-    summed = matmul(beside, values)
-    return (summed[:, :HD] / summed[:, HD:] * gates).astype(BF16)
+    summed = matmul(beside, values[...])
+    return (summed[:, :HD] / summed[:, HD:] * gates[...]).astype(BF16)
+
+
+def attend_all(queries, keys, values, gates, total, gated):
+    n = total.shape[1]
+
+    def step(index):
+        here, broad = block(index, n), block(index, HEADS * n)
+        gated[here, :] = attend(
+            queries.at[broad, :], keys.at[here, :], values.at[broad, :], gates.at[here, :], total
+        )
+
+    each(keys.shape[0] // n, n <= LANES, step)
 
 
 def bias_rows(entries, layer, ln_gain, ln_shift, w_bias, narrow):
@@ -134,54 +148,50 @@
 
 
 def bias_kernel(
-    pair_far, gain_far, shift_far, bias_far, out, normed_out, pair, ln_gain, ln_shift, w_bias, narrow, sems
+    pair_far, mask_far, chain_far, offset_far, gain_far, shift_far, bias_far, gate_far, out_far,
+    w_qkvg_far, w_out_far,
+    out, normed, known_start, known_end, pair, ln_gain, ln_shift, w_bias, gate_bias, out_bias, w_qkvg, w_out,
+    mask, chain, chain_offset, narrow, sems,
 ):
-    far, near = (pair_far, gain_far, shift_far, bias_far), (pair, ln_gain, ln_shift, w_bias)
-    for copy in fetch(zip(far, near, strict=True), sems):
-        copy.wait()
-    normed_out[...] = bias_rows(pair[...].astype(F32), 0, ln_gain, ln_shift, w_bias, narrow)
-    pack_bias(narrow, 0, out)
-
-
-def project_kernel(
-    offset_far, mask_far, chain_far, w_far, gate_far, w_out_far, out_bias_far, normed,
-    logits, values, gates, known_end, w_qkvg, gate_bias, w_out, out_bias,
-    chain_offset, mask, chain, known_start, queries, keys, sems,
-):
-    n = known_start.shape[1]
-    far = (w_far, gate_far, offset_far, mask_far, chain_far, w_out_far, out_bias_far)
-    near = (w_qkvg, gate_bias, chain_offset, mask, chain, w_out, out_bias)
-    copies = fetch(zip(far, near, strict=True), sems)
+    moves = (
+        (pair_far, pair), (mask_far, mask), (chain_far, chain), (offset_far, chain_offset),
+        (gain_far, ln_gain), (shift_far, ln_shift), (bias_far, w_bias), (gate_far, gate_bias),
+        (out_far, out_bias), (w_qkvg_far, w_qkvg), (w_out_far, w_out),
+    )
+    copies = [
+        pltpu.make_async_copy(far, near, sems.at[index]) for index, (far, near) in enumerate(moves)
+    ]
     for copy in copies:
+        copy.start()
+    for copy in copies[1:7]:
         copy.wait()
     known_logits(0, mask, chain, chain_offset, known_start)
     known_logits(1, mask, chain, chain_offset, known_end)
-
-    def row_step(row):
-        here, wide = block(row, n), block(row, HEADS * n)
-        project(
-            normed[here, :], w_qkvg[0], gate_bias[0:1, :], queries.at[wide, :], keys.at[here, :],
-            values.at[wide, :], gates.at[here, :],
-        )
-        logits[wide, :] = matmul(queries[wide, :], keys[here, :], NT) + known_start[...]
-
-    each(keys.shape[0] // n, n <= LANES, row_step)
+    copies[0].wait()
+    normed[...] = bias_rows(pair[...].astype(F32), 0, ln_gain, ln_shift, w_bias, narrow)
+    pack_bias(narrow, 0, out)
+    for copy in copies[7:]:
+        copy.wait()
 
 
 def start_kernel(
-    first_order, second_order, received, pair, logits, values, gates, ln_gain, ln_shift, w_bias, w_out,
-    out_bias, out, wide, total, gated, narrow, column, packed,
+    first_order, second_order, received, normed, pair, known, ln_gain, ln_shift, w_bias, gate_bias,
+    out_bias, w_qkvg, w_out, out, wide, total, gated, narrow, column, packed, queries, keys, values, gates,
 ):
     parts, n = out.shape[0], total.shape[1]
     rows = pair.shape[0] // n
     square = rows * rows
-    add_bias(first_order, received, 0, wide, total)
-
-    def row_step(row):
+
+    def project_step(row):
         here, broad = block(row, n), block(row, HEADS * n)
-        gated[here, :] = attend(logits[broad, :] + total[...], values[broad, :], gates[here, :])
-
-    each(rows, n <= LANES, row_step)
+        project(
+            normed[here, :], w_qkvg[0], gate_bias[0:1, :], queries.at[broad, :], keys.at[here, :],
+            values.at[broad, :], gates.at[here, :],
+        )
+
+    each(rows, n <= LANES, project_step)
+    add_bias(False, first_order, received, 0, wide, known, total)
+    attend_all(queries, keys, values, gates, total, gated)
     update = matmul(gated[...], w_out[0]) + out_bias[0:1, :]
     started = (pair[...].astype(F32) + update).astype(BF16).astype(F32)
     column[...] = started
@@ -197,10 +207,10 @@
 
 
 def end_kernel(
-    order, received, known, ln_gain, ln_shift, w_qkvg, gate_bias, w_out, out_bias, out, wide, total, gated,
+    order, received, known, ln_gain, ln_shift, gate_bias, out_bias, w_qkvg, w_out, out, wide, total, gated,
     packed, queries, keys, values, gates,
 ):
-    parts, n = received.shape[0], total.shape[1]
+    n = total.shape[1]
     rows = packed.shape[0] // n
     square = rows * rows
     for place, part in enumerate(order):
@@ -216,14 +226,8 @@
         )
 
     each(rows, n <= LANES, project_step)
-    add_bias(order, received, square, wide, total, known)
-
-    def column_step(place):
-        here, broad = block(place, n), block(place, HEADS * n)
-        logits = matmul(queries[broad, :], keys[here, :], NT) + total[...]
-        gated[here, :] = attend(logits, values[broad, :], gates[here, :])
-
-    each(rows, n <= LANES, column_step)
+    add_bias(True, order, received, square, wide, known, total)
+    attend_all(queries, keys, values, gates, total, gated)
     update = matmul(gated[...], w_out[1]) + out_bias[1:2, :]
     for place in range(rows):
         stripe = pl.ds(place, n, stride=rows)
@@ -277,53 +281,44 @@
     narrow = pltpu.VMEM((slots, n), F32)
     gated = pltpu.VMEM((rows * n, HD), BF16)
     entries = pltpu.VMEM((rows * n, C), F32)
-    bias_part, normed, *early = call(
+    parted = [
+        pltpu.VMEM((rows * HEADS * n, HD), BF16),
+        pltpu.VMEM((rows * n, HD), BF16),
+        pltpu.VMEM((rows * HEADS * n, 2 * HD), BF16),
+        pltpu.VMEM((rows * n, HD), F32),
+    ]
+    known = shape((HEADS * n, n), F32)
+    kept = (ln_gain, ln_shift, w_bias, gate_bias, out_bias, w_qkvg, w_out)
+    bias_part, normed, known_start, known_end, pair_near, *near = call(
         bias_kernel,
-        [shape((parts, tiles * slots, LANES), BF16), shape((rows * n, C), BF16)]
-        + like(flat, ln_gain, ln_shift, w_bias),
-        [narrow, pltpu.SemaphoreType.DMA((4,))],
-        (flat, ln_gain, ln_shift, w_bias),
-        (),
-    )
-    pair_near, gain_near, shift_near, bias_near = early
-    bias_all = exchange(bias_part, first_order)
-    queries, keys = ((rows * HEADS * n, HD), BF16), ((rows * n, HD), BF16)
-    values, gates = ((rows * HEADS * n, 2 * HD), BF16), ((rows * n, HD), F32)
-    late = call(
-        project_kernel,
-        [shape((rows * HEADS * n, n), F32), shape(*values), shape(*gates), shape((HEADS * n, n), F32)]
-        + like(w_qkvg, gate_bias, w_out, out_bias),
+        [shape((parts, tiles * slots, LANES), BF16), shape((rows * n, C), BF16), known, known]
+        + like(flat, *kept),
         [
-            pltpu.SMEM(chain_offset.shape, F32),
             pltpu.VMEM((1, n), jnp.int32),
             pltpu.VMEM((1, n), jnp.int32),
-            total,
-            pltpu.VMEM(*queries),
-            pltpu.VMEM(*keys),
-            pltpu.SemaphoreType.DMA((7,)),
+            pltpu.SMEM(chain_offset.shape, F32),
+            narrow,
+            pltpu.SemaphoreType.DMA((11,)),
         ],
-        (chain_offset, mask_row, chain_row, w_qkvg, gate_bias, w_out, out_bias),
-        (normed,),
-    )
-    *projected, known_end, w_near, gate_near, w_out_near, out_near = late
+        (flat, mask_row, chain_row, chain_offset, *kept),
+        (),
+    )
+    bias_all = exchange(bias_part, first_order)
     sent = call(
         functools.partial(start_kernel, first_order, second_order),
         shape((parts, square + tiles * slots, LANES), BF16),
-        [wide, total, gated, narrow, entries, entries],
+        [wide, total, gated, narrow, entries, entries, *parted],
         (),
-        (
-            bias_all, pair_near, *projected, gain_near, shift_near, bias_near, w_out_near, out_near
-        ),
+        (bias_all, normed, pair_near, known_start, *near),
     )
     columns = exchange(sent, second_order)
+    gain_near, shift_near, _, *near = near
     ended = call(
         functools.partial(end_kernel, second_order),
         shape((n * rows, C), BF16),
-        [wide, total, gated, entries] + [pltpu.VMEM(*each_one) for each_one in (queries, keys, values, gates)],
+        [wide, total, gated, entries, *parted],
         (),
-        (
-            columns, known_end, gain_near, shift_near, w_near, gate_near, w_out_near, out_near
-        ),
+        (columns, known_end, gain_near, shift_near, *near),
     )
     return ended.reshape(n, rows, C)
 

time: 32.5 us -> 32.1 us (0.988)
  blocking collectives: 12.1 us -> 27.1 us
  starting transfers between devices: 7.3 us -> 0 us
  waiting for transfers between devices: 6.04 us -> 0 us
  Pallas kernels: 6.82 us -> 4.85 us
    all_to_all x1 -> x2, blocking collectives: 12.1 us -> 27.1 us  [exchange(): lax.all_to_all(array, ('row', 'sub'), split_axis=0, concat_axis=0, tiled=...]
    all_to_all x1 -> x0, starting transfers between devices: 7.3 us -> none  [exchange(): lax.all_to_all(array, ('row', 'sub'), split_axis=0, concat_axis=0, tiled=...]
    all_to_all x1 -> x0, waiting for transfers between devices: 6.04 us -> none  [exchange(): lax.all_to_all(array, ('row', 'sub'), split_axis=0, concat_axis=0, tiled=...]
    pallas_call x4 -> x3, Pallas kernels: 6.82 us -> 4.85 us  [call(): pl.pallas_call(kernel, out_shape=out_shape, in_specs=[FAR] * len(far) + [...]
  transfers between devices with their start and end apart: 1 -> 0, of which waited for: 1 -> 0; matrix products, arithmetic and copies ran while one was open for 0% -> 0% of each run, Pallas kernels for 6% -> 0%
where the time goes in v5:
time: 32.1 us; the launch traced here: 31.9 us
  blocking collectives  27.1 us (84%)
  Pallas kernels  4.85 us (15%)
    all_to_all x2, blocking collectives, exchange(): lax.all_to_all(array, ('row', 'sub'), split_axis=0, concat_axis=0, tiled=...  27.1 us
    pallas_call x3, Pallas kernels, call(): pl.pallas_call(kernel, out_shape=out_shape, in_specs=[FAR] * len(far) + [...  4.85 us

profile of v5, /device:TPU:0, one launch (start us, length us, event | category | flops | bytes accessed | tf_op | source)
XLA Modules:
  0.0 31.9 jit_solution(16063226334558147573)
XLA Ops:
  0.0 1.4 %shard_map.109 = (bf16[32,16,128]{2,1,0:T(8,128)(2,1)S(1)}, bf16[512,128]{1,0:T(8,128)(2,1)S(1)}, f32[512,128]{1,0:T(8,128)S(1)}, f32[512,128]{1,0:T(8,128)S(1)}...) custom-call(bf16[512,128]{1,0:T(8,128)(2,1)} %bitcast.4, ...), custom_call_target="tpu_custom_call" | custom-call | tf_op jit(solution)/shard_map/pallas_call | solution.py:244
  1.4 14.9 %all_to_all.10.received = bf16[32,16,128]{2,1,0:T(8,128)(2,1)S(1)} all-to-all(bf16[32,16,128]{2,1,0:T(8,128)(2,1)S(1)} %get-tuple-element.17), channel_id=1, replica_groups={{31,30,29,28,27,26,25,24,23,22,21,20,19,18,17,16,15,14,13,12,11,10,9,8,..., dimensions={0} | all-to-all | bytes 262144 | tf_op jit(solution)/shard_map/all_to_all | solution.py:255
  16.4 1.4 %shard_map.110 = bf16[32,32,128]{2,1,0:T(8,128)(2,1)S(1)} custom-call(bf16[32,16,128]{2,1,0:T(8,128)(2,1)S(1)} %all_to_all.10.received, bf16[512,128]{1,0:T(8,128)(2,1)S(1)} %get-tuple-element.18.normed, bf16[512,128]{1,0:T(8,128)(2,1)S(1)} %get-tuple-element.19.pair, f32[512,128]{1,0:T(8,128)S(1)} %get-tuple-element.20.known, ...), custom_call_target="tpu_custom_call" | custom-call | tf_op jit(solution)/shard_map/pallas_call | solution.py:244
  17.8 12.1 %all_to_all.11.received = bf16[32,32,128]{2,1,0:T(8,128)(2,1)S(1)} all-to-all(bf16[32,32,128]{2,1,0:T(8,128)(2,1)S(1)} %shard_map.110), channel_id=1, replica_groups={{0,1,2,3,4,5,6,7,8,9,10,11,12,13,14,15,16,17,18,19,20,21,22,23,24,25,26..., dimensions={0} | all-to-all | bytes 524288 | tf_op jit(solution)/shard_map/all_to_all | solution.py:255
  29.9 2.1 %shard_map.111 = bf16[512,128]{1,0:T(8,128)(2,1)} custom-call(bf16[32,32,128]{2,1,0:T(8,128)(2,1)S(1)} %all_to_all.11.received, f32[512,128]{1,0:T(8,128)S(1)} %get-tuple-element.28.known, f32[2,128]{1,0:T(2,128)S(1)} %get-tuple-element.21.ln_gain, f32[2,128]{1,0:T(2,128)S(1)} %get-tuple-element.22.ln_shift, f32[2,128]{1,0:T(2,128)S(1)} %get-tuple-element.24.gate_bias, ...), custom_call_target="tpu_custom_call" | custom-call | tf_op jit(solution)/shard_map/pallas_call | solution.py:244

commit v6 on v5

--- a/solution.py
+++ b/solution.py
@@ -33,7 +33,7 @@
 
 def head_mask(head):
     lane = lax.broadcasted_iota(jnp.int32, (1, HD), 1)
-    return jnp.where(lane // HEAD_DIM == head, 1.0, 0.0).astype(F32)
+    return jnp.where(lane // HEAD_DIM == head, 1.0, 0.0).astype(BF16)
 
 
 def each(count, unrolled, body):
@@ -87,15 +87,15 @@
 def project(normed, weights, gate_row, queries, keys, values, gates):
     n = normed.shape[0]
     projected = matmul(normed, weights)
-    scaled = projected[:, :HD] * (HEAD_DIM ** (-0.5))
+    scaled = (projected[:, :HD] * (HEAD_DIM ** (-0.5))).astype(BF16)
     keys[...] = projected[:, HD : 2 * HD].astype(BF16)
-    held = projected[:, 2 * HD : 3 * HD]
+    held = projected[:, 2 * HD : 3 * HD].astype(BF16)
     gates[...] = jax.nn.sigmoid(projected[:, 3 * HD :].astype(BF16).astype(F32) + gate_row)
     for head in range(HEADS):
         own = head_mask(head)
-        queries[block(head, n), :] = (scaled * own).astype(BF16)
-        values[block(head, n), :HD] = (held * own).astype(BF16)
-        values[block(head, n), HD:] = jnp.broadcast_to(own.astype(BF16), (n, HD))
+        queries[block(head, n), :] = scaled * own
+        values[block(head, n), :HD] = held * own
+        values[block(head, n), HD:] = jnp.broadcast_to(own, (n, HD))
 
 
 def attend(queries, keys, values, gates, total):
@@ -259,7 +259,14 @@
 
 def orders(outer, inner):
     natural = list(range(outer * inner))
-    return natural[::-1], natural
+    pair = 2 if outer % 2 == 0 else 1
+    apart = [
+        (place * pair + half) * inner + part
+        for half in range(pair)
+        for part in range(inner)
+        for place in range(outer // pair)
+    ]
+    return natural[::-1], apart[::-1]
 
 
 def local(

time: 32.1 us -> 31.6 us (0.984)
  blocking collectives: 27.1 us -> 26.6 us
    all_to_all x2, blocking collectives: 27.1 us -> 26.6 us  [exchange(): lax.all_to_all(array, ('row', 'sub'), split_axis=0, concat_axis=0, tiled=...]
where the time goes in v6:
time: 31.6 us; the launch traced here: 31.4 us
  blocking collectives  26.6 us (84%)
  Pallas kernels  4.77 us (15%)
    all_to_all x2, blocking collectives, exchange(): lax.all_to_all(array, ('row', 'sub'), split_axis=0, concat_axis=0, tiled=...  26.6 us
    pallas_call x3, Pallas kernels, call(): pl.pallas_call(kernel, out_shape=out_shape, in_specs=[FAR] * len(far) + [...  4.77 us

profile of v6, /device:TPU:0, one launch (start us, length us, event | category | flops | bytes accessed | tf_op | source)
XLA Modules:
  0.0 31.4 jit_solution(2659239092261809572)
XLA Ops:
  0.0 1.4 %shard_map.109 = (bf16[32,16,128]{2,1,0:T(8,128)(2,1)S(1)}, bf16[512,128]{1,0:T(8,128)(2,1)S(1)}, f32[512,128]{1,0:T(8,128)S(1)}, f32[512,128]{1,0:T(8,128)S(1)}...) custom-call(bf16[512,128]{1,0:T(8,128)(2,1)} %bitcast.4, ...), custom_call_target="tpu_custom_call" | custom-call | tf_op jit(solution)/shard_map/pallas_call | solution.py:244
  1.4 14.9 %all_to_all.10.received = bf16[32,16,128]{2,1,0:T(8,128)(2,1)S(1)} all-to-all(bf16[32,16,128]{2,1,0:T(8,128)(2,1)S(1)} %get-tuple-element.17), channel_id=1, replica_groups={{31,30,29,28,27,26,25,24,23,22,21,20,19,18,17,16,15,14,13,12,11,10,9,8,..., dimensions={0} | all-to-all | bytes 262144 | tf_op jit(solution)/shard_map/all_to_all | solution.py:255
  16.4 1.3 %shard_map.110 = bf16[32,32,128]{2,1,0:T(8,128)(2,1)S(1)} custom-call(bf16[32,16,128]{2,1,0:T(8,128)(2,1)S(1)} %all_to_all.10.received, bf16[512,128]{1,0:T(8,128)(2,1)S(1)} %get-tuple-element.18.normed, bf16[512,128]{1,0:T(8,128)(2,1)S(1)} %get-tuple-element.19.pair, f32[512,128]{1,0:T(8,128)S(1)} %get-tuple-element.20.known, ...), custom_call_target="tpu_custom_call" | custom-call | tf_op jit(solution)/shard_map/pallas_call | solution.py:244
  17.7 11.6 %all_to_all.11.received = bf16[32,32,128]{2,1,0:T(8,128)(2,1)S(1)} all-to-all(bf16[32,32,128]{2,1,0:T(8,128)(2,1)S(1)} %shard_map.110), channel_id=1, replica_groups={{31,23,15,7,30,22,14,6,29,21,13,5,28,20,12,4,27,19,11,3,26,18,10,2,25,1..., dimensions={0} | all-to-all | bytes 524288 | tf_op jit(solution)/shard_map/all_to_all | solution.py:255
  29.3 2.0 %shard_map.111 = bf16[512,128]{1,0:T(8,128)(2,1)} custom-call(bf16[32,32,128]{2,1,0:T(8,128)(2,1)S(1)} %all_to_all.11.received, f32[512,128]{1,0:T(8,128)S(1)} %get-tuple-element.28.known, f32[2,128]{1,0:T(2,128)S(1)} %get-tuple-element.21.ln_gain, f32[2,128]{1,0:T(2,128)S(1)} %get-tuple-element.22.ln_shift, f32[2,128]{1,0:T(2,128)S(1)} %get-tuple-element.24.gate_bias, ...), custom_call_target="tpu_custom_call" | custom-call | tf_op jit(solution)/shard_map/pallas_call | solution.py:244

commit v7 on v6

--- a/solution.py
+++ b/solution.py
@@ -94,17 +94,17 @@
     for head in range(HEADS):
         own = head_mask(head)
         queries[block(head, n), :] = scaled * own
-        values[block(head, n), :HD] = held * own
-        values[block(head, n), HD:] = jnp.broadcast_to(own, (n, HD))
+        values[block(head, n), :] = held * own
 
 
 def attend(queries, keys, values, gates, total):
     n = keys.shape[0]
     logits = matmul(queries[...], keys[...], NT) + total[...]
-    expon = jnp.exp(logits - jnp.max(logits, axis=-1, keepdims=True)).astype(BF16)
-    beside = jnp.concatenate([expon[block(head, n), :] for head in range(HEADS)], axis=1)
+    expon = jnp.exp(logits - jnp.max(logits, axis=-1, keepdims=True))
+    weights = (expon / jnp.sum(expon, axis=-1, keepdims=True)).astype(BF16)
+    beside = jnp.concatenate([weights[block(head, n), :] for head in range(HEADS)], axis=1)
     summed = matmul(beside, values[...])
-    return (summed[:, :HD] / summed[:, HD:] * gates[...]).astype(BF16)
+    return (summed * gates[...]).astype(BF16)
 
 
 def attend_all(queries, keys, values, gates, total, gated):
@@ -291,7 +291,7 @@
     parted = [
         pltpu.VMEM((rows * HEADS * n, HD), BF16),
         pltpu.VMEM((rows * n, HD), BF16),
-        pltpu.VMEM((rows * HEADS * n, 2 * HD), BF16),
+        pltpu.VMEM((rows * HEADS * n, HD), BF16),
         pltpu.VMEM((rows * n, HD), F32),
     ]
     known = shape((HEADS * n, n), F32)

time: 31.6 us -> 32.2 us (1.019)
  Pallas kernels: 4.77 us -> 5.32 us
    pallas_call x3, Pallas kernels: 4.77 us -> 5.32 us  [call(): pl.pallas_call(kernel, out_shape=out_shape, in_specs=[FAR] * len(far) + [...]
where the time goes in v7:
time: 32.2 us; the launch traced here: 31.9 us
  blocking collectives  26.6 us (83%)
  Pallas kernels  5.32 us (17%)
    all_to_all x2, blocking collectives, exchange(): lax.all_to_all(array, ('row', 'sub'), split_axis=0, concat_axis=0, tiled=...  26.6 us
    pallas_call x3, Pallas kernels, call(): pl.pallas_call(kernel, out_shape=out_shape, in_specs=[FAR] * len(far) + [...  5.32 us

profile of v7, /device:TPU:0, one launch (start us, length us, event | category | flops | bytes accessed | tf_op | source)
XLA Modules:
  0.0 31.9 jit_solution(3369768922914390105)
XLA Ops:
  0.0 1.4 %shard_map.109 = (bf16[32,16,128]{2,1,0:T(8,128)(2,1)S(1)}, bf16[512,128]{1,0:T(8,128)(2,1)S(1)}, f32[512,128]{1,0:T(8,128)S(1)}, f32[512,128]{1,0:T(8,128)S(1)}...) custom-call(bf16[512,128]{1,0:T(8,128)(2,1)} %bitcast.4, ...), custom_call_target="tpu_custom_call" | custom-call | tf_op jit(solution)/shard_map/pallas_call | solution.py:244
  1.4 14.9 %all_to_all.10.received = bf16[32,16,128]{2,1,0:T(8,128)(2,1)S(1)} all-to-all(bf16[32,16,128]{2,1,0:T(8,128)(2,1)S(1)} %get-tuple-element.17), channel_id=1, replica_groups={{31,30,29,28,27,26,25,24,23,22,21,20,19,18,17,16,15,14,13,12,11,10,9,8,..., dimensions={0} | all-to-all | bytes 262144 | tf_op jit(solution)/shard_map/all_to_all | solution.py:255
  16.4 1.6 %shard_map.110 = bf16[32,32,128]{2,1,0:T(8,128)(2,1)S(1)} custom-call(bf16[32,16,128]{2,1,0:T(8,128)(2,1)S(1)} %all_to_all.10.received, bf16[512,128]{1,0:T(8,128)(2,1)S(1)} %get-tuple-element.18.normed, bf16[512,128]{1,0:T(8,128)(2,1)S(1)} %get-tuple-element.19.pair, f32[512,128]{1,0:T(8,128)S(1)} %get-tuple-element.20.known, ...), custom_call_target="tpu_custom_call" | custom-call | tf_op jit(solution)/shard_map/pallas_call | solution.py:244
  18.0 11.6 %all_to_all.11.received = bf16[32,32,128]{2,1,0:T(8,128)(2,1)S(1)} all-to-all(bf16[32,32,128]{2,1,0:T(8,128)(2,1)S(1)} %shard_map.110), channel_id=1, replica_groups={{31,23,15,7,30,22,14,6,29,21,13,5,28,20,12,4,27,19,11,3,26,18,10,2,25,1..., dimensions={0} | all-to-all | bytes 524288 | tf_op jit(solution)/shard_map/all_to_all | solution.py:255
  29.7 2.3 %shard_map.111 = bf16[512,128]{1,0:T(8,128)(2,1)} custom-call(bf16[32,32,128]{2,1,0:T(8,128)(2,1)S(1)} %all_to_all.11.received, f32[512,128]{1,0:T(8,128)S(1)} %get-tuple-element.28.known, f32[2,128]{1,0:T(2,128)S(1)} %get-tuple-element.21.ln_gain, f32[2,128]{1,0:T(2,128)S(1)} %get-tuple-element.22.ln_shift, f32[2,128]{1,0:T(2,128)S(1)} %get-tuple-element.24.gate_bias, ...), custom_call_target="tpu_custom_call" | custom-call | tf_op jit(solution)/shard_map/pallas_call | solution.py:244

commit v8 on v7

--- a/solution.py
+++ b/solution.py
@@ -84,8 +84,8 @@
                 total[here, span] = gathered + known[here, span]
 
 
-def project(normed, weights, gate_row, queries, keys, values, gates):
-    n = normed.shape[0]
+def project(normed, weights, gate_row, queries, keys, values, gates, n):
+    count = normed.shape[0] // n
     projected = matmul(normed, weights)
     scaled = (projected[:, :HD] * (HEAD_DIM ** (-0.5))).astype(BF16)
     keys[...] = projected[:, HD : 2 * HD].astype(BF16)
@@ -93,8 +93,10 @@
     gates[...] = jax.nn.sigmoid(projected[:, 3 * HD :].astype(BF16).astype(F32) + gate_row)
     for head in range(HEADS):
         own = head_mask(head)
-        queries[block(head, n), :] = scaled * own
-        values[block(head, n), :] = held * own
+        own_queries, own_values = scaled * own, held * own
+        for row in range(count):
+            queries[block(row * HEADS + head, n), :] = own_queries[block(row, n), :]
+            values[block(row * HEADS + head, n), :] = own_values[block(row, n), :]
 
 
 def attend(queries, keys, values, gates, total):
@@ -182,15 +184,8 @@
     rows = pair.shape[0] // n
     square = rows * rows
 
-    def project_step(row):
-        here, broad = block(row, n), block(row, HEADS * n)
-        project(
-            normed[here, :], w_qkvg[0], gate_bias[0:1, :], queries.at[broad, :], keys.at[here, :],
-            values.at[broad, :], gates.at[here, :],
-        )
-
-    each(rows, n <= LANES, project_step)
     add_bias(False, first_order, received, 0, wide, known, total)
+    project(normed[...], w_qkvg[0], gate_bias[0:1, :], queries, keys, values, gates, n)
     attend_all(queries, keys, values, gates, total, gated)
     update = matmul(gated[...], w_out[0]) + out_bias[0:1, :]
     started = (pair[...].astype(F32) + update).astype(BF16).astype(F32)
@@ -216,17 +211,10 @@
     for place, part in enumerate(order):
         packed[block(part, square), :] = received[place, :square, :].astype(F32)
 
-    def project_step(place):
-        here, broad = block(place, n), block(place, HEADS * n)
-        entries = packed[pl.ds(place, n, stride=rows), :]
-        normed = layer_norm(entries, ln_gain[1:2, :], ln_shift[1:2, :])
-        project(
-            normed, w_qkvg[1], gate_bias[1:2, :], queries.at[broad, :], keys.at[here, :],
-            values.at[broad, :], gates.at[here, :],
-        )
-
-    each(rows, n <= LANES, project_step)
     add_bias(True, order, received, square, wide, known, total)
+    entries = jnp.concatenate([packed[pl.ds(place, n, stride=rows), :] for place in range(rows)], axis=0)
+    normed = layer_norm(entries, ln_gain[1:2, :], ln_shift[1:2, :])
+    project(normed, w_qkvg[1], gate_bias[1:2, :], queries, keys, values, gates, n)
     attend_all(queries, keys, values, gates, total, gated)
     update = matmul(gated[...], w_out[1]) + out_bias[1:2, :]
     for place in range(rows):

time: 32.2 us -> 32.1 us (level)
  no operation moved by 1% of the time
where the time goes in v8:
time: 32.1 us; the launch traced here: 31.9 us
  blocking collectives  26.6 us (83%)
  Pallas kernels  5.28 us (16%)
    all_to_all x2, blocking collectives, exchange(): lax.all_to_all(array, ('row', 'sub'), split_axis=0, concat_axis=0, tiled=...  26.6 us
    pallas_call x3, Pallas kernels, call(): pl.pallas_call(kernel, out_shape=out_shape, in_specs=[FAR] * len(far) + [...  5.28 us

profile of v8, /device:TPU:0, one launch (start us, length us, event | category | flops | bytes accessed | tf_op | source)
XLA Modules:
  0.0 31.9 jit_solution(6831671991009186944)
XLA Ops:
  0.0 1.4 %shard_map.109 = (bf16[32,16,128]{2,1,0:T(8,128)(2,1)S(1)}, bf16[512,128]{1,0:T(8,128)(2,1)S(1)}, f32[512,128]{1,0:T(8,128)S(1)}, f32[512,128]{1,0:T(8,128)S(1)}...) custom-call(bf16[512,128]{1,0:T(8,128)(2,1)} %bitcast.4, ...), custom_call_target="tpu_custom_call" | custom-call | tf_op jit(solution)/shard_map/pallas_call | solution.py:232
  1.4 14.9 %all_to_all.10.received = bf16[32,16,128]{2,1,0:T(8,128)(2,1)S(1)} all-to-all(bf16[32,16,128]{2,1,0:T(8,128)(2,1)S(1)} %get-tuple-element.17), channel_id=1, replica_groups={{31,30,29,28,27,26,25,24,23,22,21,20,19,18,17,16,15,14,13,12,11,10,9,8,..., dimensions={0} | all-to-all | bytes 262144 | tf_op jit(solution)/shard_map/all_to_all | solution.py:243
  16.4 1.6 %shard_map.110 = bf16[32,32,128]{2,1,0:T(8,128)(2,1)S(1)} custom-call(bf16[32,16,128]{2,1,0:T(8,128)(2,1)S(1)} %all_to_all.10.received, bf16[512,128]{1,0:T(8,128)(2,1)S(1)} %get-tuple-element.18.normed, bf16[512,128]{1,0:T(8,128)(2,1)S(1)} %get-tuple-element.19.pair, f32[512,128]{1,0:T(8,128)S(1)} %get-tuple-element.20.known, ...), custom_call_target="tpu_custom_call" | custom-call | tf_op jit(solution)/shard_map/pallas_call | solution.py:232
  18.0 11.6 %all_to_all.11.received = bf16[32,32,128]{2,1,0:T(8,128)(2,1)S(1)} all-to-all(bf16[32,32,128]{2,1,0:T(8,128)(2,1)S(1)} %shard_map.110), channel_id=1, replica_groups={{31,23,15,7,30,22,14,6,29,21,13,5,28,20,12,4,27,19,11,3,26,18,10,2,25,1..., dimensions={0} | all-to-all | bytes 524288 | tf_op jit(solution)/shard_map/all_to_all | solution.py:243
  29.7 2.2 %shard_map.111 = bf16[512,128]{1,0:T(8,128)(2,1)} custom-call(bf16[32,32,128]{2,1,0:T(8,128)(2,1)S(1)} %all_to_all.11.received, f32[512,128]{1,0:T(8,128)S(1)} %get-tuple-element.28.known, f32[2,128]{1,0:T(2,128)S(1)} %get-tuple-element.21.ln_gain, f32[2,128]{1,0:T(2,128)S(1)} %get-tuple-element.22.ln_shift, f32[2,128]{1,0:T(2,128)S(1)} %get-tuple-element.24.gate_bias, ...), custom_call_target="tpu_custom_call" | custom-call | tf_op jit(solution)/shard_map/pallas_call | solution.py:232

commit v9 on v8

--- a/solution.py
+++ b/solution.py
@@ -90,7 +90,8 @@
     scaled = (projected[:, :HD] * (HEAD_DIM ** (-0.5))).astype(BF16)
     keys[...] = projected[:, HD : 2 * HD].astype(BF16)
     held = projected[:, 2 * HD : 3 * HD].astype(BF16)
-    gates[...] = jax.nn.sigmoid(projected[:, 3 * HD :].astype(BF16).astype(F32) + gate_row)
+    gate_logits = projected[:, 3 * HD :].astype(BF16).astype(F32) + gate_row
+    gates[...] = 0.5 * jnp.tanh(0.5 * gate_logits) + 0.5
     for head in range(HEADS):
         own = head_mask(head)
         own_queries, own_values = scaled * own, held * own
@@ -165,13 +166,12 @@
     ]
     for copy in copies:
         copy.start()
-    for copy in copies[1:7]:
+    for copy in copies[:7]:
         copy.wait()
+    normed[...] = bias_rows(pair[...].astype(F32), 0, ln_gain, ln_shift, w_bias, narrow)
+    pack_bias(narrow, 0, out)
     known_logits(0, mask, chain, chain_offset, known_start)
     known_logits(1, mask, chain, chain_offset, known_end)
-    copies[0].wait()
-    normed[...] = bias_rows(pair[...].astype(F32), 0, ln_gain, ln_shift, w_bias, narrow)
-    pack_bias(narrow, 0, out)
     for copy in copies[7:]:
         copy.wait()
 
@@ -219,7 +219,7 @@
     update = matmul(gated[...], w_out[1]) + out_bias[1:2, :]
     for place in range(rows):
         stripe = pl.ds(place, n, stride=rows)
-        packed[stripe, :] = packed[stripe, :] + update[block(place, n), :]
+        packed[stripe, :] = entries[block(place, n), :] + update[block(place, n), :]
     out[...] = packed[...].astype(BF16)
 
 

time: 32.1 us -> 32.1 us (level)
  no operation moved by 1% of the time
where the time goes in v9:
time: 32.1 us; the launch traced here: 31.9 us
  blocking collectives  26.6 us (83%)
  Pallas kernels  5.25 us (16%)
    all_to_all x2, blocking collectives, exchange(): lax.all_to_all(array, ('row', 'sub'), split_axis=0, concat_axis=0, tiled=...  26.6 us
    pallas_call x3, Pallas kernels, call(): pl.pallas_call(kernel, out_shape=out_shape, in_specs=[FAR] * len(far) + [...  5.25 us

profile of v9, /device:TPU:0, one launch (start us, length us, event | category | flops | bytes accessed | tf_op | source)
XLA Modules:
  0.0 31.9 jit_solution(4651566459700218690)
XLA Ops:
  0.0 1.4 %shard_map.109 = (bf16[32,16,128]{2,1,0:T(8,128)(2,1)S(1)}, bf16[512,128]{1,0:T(8,128)(2,1)S(1)}, f32[512,128]{1,0:T(8,128)S(1)}, f32[512,128]{1,0:T(8,128)S(1)}...) custom-call(bf16[512,128]{1,0:T(8,128)(2,1)} %bitcast.4, ...), custom_call_target="tpu_custom_call" | custom-call | tf_op jit(solution)/shard_map/pallas_call | solution.py:232
  1.4 14.9 %all_to_all.10.received = bf16[32,16,128]{2,1,0:T(8,128)(2,1)S(1)} all-to-all(bf16[32,16,128]{2,1,0:T(8,128)(2,1)S(1)} %get-tuple-element.17), channel_id=1, replica_groups={{31,30,29,28,27,26,25,24,23,22,21,20,19,18,17,16,15,14,13,12,11,10,9,8,..., dimensions={0} | all-to-all | bytes 262144 | tf_op jit(solution)/shard_map/all_to_all | solution.py:243
  16.3 1.6 %shard_map.110 = bf16[32,32,128]{2,1,0:T(8,128)(2,1)S(1)} custom-call(bf16[32,16,128]{2,1,0:T(8,128)(2,1)S(1)} %all_to_all.10.received, bf16[512,128]{1,0:T(8,128)(2,1)S(1)} %get-tuple-element.18.normed, bf16[512,128]{1,0:T(8,128)(2,1)S(1)} %get-tuple-element.19.pair, f32[512,128]{1,0:T(8,128)S(1)} %get-tuple-element.20.known, ...), custom_call_target="tpu_custom_call" | custom-call | tf_op jit(solution)/shard_map/pallas_call | solution.py:232
  18.0 11.6 %all_to_all.11.received = bf16[32,32,128]{2,1,0:T(8,128)(2,1)S(1)} all-to-all(bf16[32,32,128]{2,1,0:T(8,128)(2,1)S(1)} %shard_map.110), channel_id=1, replica_groups={{31,23,15,7,30,22,14,6,29,21,13,5,28,20,12,4,27,19,11,3,26,18,10,2,25,1..., dimensions={0} | all-to-all | bytes 524288 | tf_op jit(solution)/shard_map/all_to_all | solution.py:243
  29.6 2.2 %shard_map.111 = bf16[512,128]{1,0:T(8,128)(2,1)} custom-call(bf16[32,32,128]{2,1,0:T(8,128)(2,1)S(1)} %all_to_all.11.received, f32[512,128]{1,0:T(8,128)S(1)} %get-tuple-element.28.known, f32[2,128]{1,0:T(2,128)S(1)} %get-tuple-element.21.ln_gain, f32[2,128]{1,0:T(2,128)S(1)} %get-tuple-element.22.ln_shift, f32[2,128]{1,0:T(2,128)S(1)} %get-tuple-element.24.gate_bias, ...), custom_call_target="tpu_custom_call" | custom-call | tf_op jit(solution)/shard_map/pallas_call | solution.py:232
